TPU v7x, 32 devices: a whole 2x2x4 slice. The times are simulated.
32 devices in a mesh: ctx: 16 (over z, y, x), fsdp: 2 (over core).
Axes of the slice: x: 2, y: 2, z: 4, core: 2. Of those that a mesh axis runs over, the one named last changes fastest.
Arguments:
- x_in: bfloat16 [4, 1024, 576], P('fsdp', 'ctx')
- w_query: bfloat16 [576, 576], P('fsdp'), may hold values from -0.25 to 0.25
- w_key: bfloat16 [576, 192], P('fsdp'), may hold values from -0.25 to 0.25
- w_value: bfloat16 [576, 192], P('fsdp'), may hold values from -0.25 to 0.25
- w_out: bfloat16 [576, 576], P('fsdp'), may hold values from -6 to 6
- attn_gain: bfloat16 [576], P('fsdp'), may hold values from 0.5 to 1.5
- w_gate: bfloat16 [576, 1536], P('fsdp'), may hold values from -0.25 to 0.25
- w_up: bfloat16 [576, 1536], P('fsdp'), may hold values from -0.25 to 0.25
- w_down: bfloat16 [1536, 576], P('fsdp'), may hold values from -0.15625 to 0.15625
- mlp_gain: bfloat16 [576], P('fsdp'), may hold values from 0.5 to 1.5
- block_of_slot: int32 [32], replicated, may hold values from 0 to 31, as said below
- out_grad: bfloat16 [4, 1024, 576], P('fsdp', 'ctx'), may hold values from -6 to 6
Outputs:
- y_out: bfloat16 [4, 1024, 576], P('fsdp', 'ctx')
- x_grad: bfloat16 [4, 1024, 576], P('fsdp', 'ctx')
- grad_w_query: float32 [576, 576], P('fsdp')
- grad_w_key: float32 [576, 192], P('fsdp')
- grad_w_value: float32 [576, 192], P('fsdp')
- grad_w_out: float32 [576, 576], P('fsdp')
- grad_attn_gain: float32 [576], P('fsdp')
- grad_w_gate: float32 [576, 1536], P('fsdp')
- grad_w_up: float32 [576, 1536], P('fsdp')
- grad_w_down: float32 [1536, 576], P('fsdp')
- grad_mlp_gain: float32 [576], P('fsdp')
Inputs may be any that keep to these rules, and one draw needn't show every extreme that they name: `block_of_slot`: the entries are a permutation of 0 to 31 and entries 2 i and 2 i + 1 sum to 31, so slots 2 i and 2 i + 1 hold a block from the front of the sequence and its mirror from the back.
All inputs are finite; a program needn't handle non-finite values.
Results may differ from a plain program's by a relative error of at most 0.025.
Values may be sent and summed in bfloat16 or wider, within the bound.
A program may use at most 128 MiB of HBM per device.

v0:
```python
import jax
import jax.numpy as jnp
from jax import lax
from jax.sharding import PartitionSpec as P

HEADS = 9
KV_HEADS = 3
HEAD_DIM = 64
epsilon = 1e-05
theta_base = 100000.0
masked_value = -1e30


def shifted(block, axis, distance):
    devices = range(lax.axis_size(axis))
    route = [((i - distance) % len(devices), i) for i in devices]
    return lax.ppermute(block, axis, route)


def make_tables(positions):
    half_dim = HEAD_DIM // 2
    frequency = theta_base ** (-2.0 * jnp.arange(half_dim, dtype=jnp.float32) / HEAD_DIM)
    angles = positions.astype(jnp.float32)[:, None] * frequency[None, :]
    return (jnp.cos(angles), jnp.sin(angles))


def rotate(values, cosine, sine):
    half_dim = values.shape[-1] // 2
    first_half = values[..., :half_dim]
    second_half = values[..., half_dim:]
    cos_rows = cosine[:, None, :]
    sin_rows = sine[:, None, :]
    return jnp.concatenate(
        [
            first_half * cos_rows - second_half * sin_rows,
            second_half * cos_rows + first_half * sin_rows,
        ],
        axis=-1,
    )


def rotate_back(grads, cosine, sine):
    half_dim = grads.shape[-1] // 2
    first_half = grads[..., :half_dim]
    second_half = grads[..., half_dim:]
    cos_rows = cosine[:, None, :]
    sin_rows = sine[:, None, :]
    return jnp.concatenate(
        [
            first_half * cos_rows + second_half * sin_rows,
            second_half * cos_rows - first_half * sin_rows,
        ],
        axis=-1,
    )


def slot_positions(block_of_slot, offset, count_rows, half_len):
    row_ids = offset + jnp.arange(count_rows, dtype=jnp.int32)
    slot_ids = row_ids // half_len
    slot_match = slot_ids[:, None] == jnp.arange(block_of_slot.shape[0], dtype=jnp.int32)[None, :]
    owners = jnp.sum(jnp.where(slot_match, block_of_slot[None, :], 0), axis=1)
    return owners * half_len + row_ids % half_len


def norm_forward(values, gain_vec):
    inverse = lax.rsqrt(jnp.mean(values * values, axis=-1, keepdims=True) + epsilon)
    scaled = values * inverse
    return (scaled * gain_vec, scaled, inverse)


def norm_backward(grad_output, gain_vec, scaled, inverse):
    grad_scaled = grad_output * gain_vec
    grad_input = inverse * (
        grad_scaled - scaled * jnp.mean(grad_scaled * scaled, axis=-1, keepdims=True)
    )
    grad_gain = jnp.sum(grad_output * scaled, axis=0)
    return (grad_input, grad_gain)


def local(
    x_in,
    w_query,
    w_key,
    w_value,
    w_out,
    attn_gain,
    w_gate,
    w_up,
    w_down,
    mlp_gain,
    block_of_slot,
    out_grad,
):
    gathered = (
        lax.all_gather(w_query, "fsdp", axis=0, tiled=True),
        lax.all_gather(w_key, "fsdp", axis=0, tiled=True),
        lax.all_gather(w_value, "fsdp", axis=0, tiled=True),
        lax.all_gather(w_out, "fsdp", axis=0, tiled=True),
        lax.all_gather(attn_gain, "fsdp", axis=0, tiled=True),
        lax.all_gather(w_gate, "fsdp", axis=0, tiled=True),
        lax.all_gather(w_up, "fsdp", axis=0, tiled=True),
        lax.all_gather(w_down, "fsdp", axis=0, tiled=True),
        lax.all_gather(mlp_gain, "fsdp", axis=0, tiled=True),
    )
    (
        full_query,
        full_key,
        full_value,
        full_out,
        gain_attn,
        full_gate,
        full_up,
        full_down,
        gain_mlp,
    ) = gathered
    gain_attn_f = gain_attn.astype(jnp.float32)
    gain_mlp_f = gain_mlp.astype(jnp.float32)
    seq_count, tok_count, model_width = x_in.shape
    group_size = HEADS // KV_HEADS
    half_len = tok_count // 2
    rows_all = seq_count * tok_count
    ctx_count = lax.axis_size("ctx")
    score_scale = HEAD_DIM ** (-0.5)
    my_offset = lax.axis_index("ctx") * tok_count
    query_pos = slot_positions(block_of_slot, my_offset, tok_count, half_len)
    cosine, sine = make_tables(query_pos)
    inputs = x_in.astype(jnp.float32).reshape(rows_all, model_width)
    normed_f, scaled_one, inverse_one = norm_forward(inputs, gain_attn_f)
    normed = normed_f.astype(jnp.bfloat16)
    query_f = jnp.dot(normed, full_query, preferred_element_type=jnp.float32).reshape(
        seq_count, tok_count, HEADS, HEAD_DIM
    )
    queries = (
        rotate(query_f, cosine, sine)
        .astype(jnp.bfloat16)
        .reshape(seq_count, tok_count, KV_HEADS, group_size, HEAD_DIM)
    )
    key_f = jnp.dot(normed, full_key, preferred_element_type=jnp.float32).reshape(
        seq_count, tok_count, KV_HEADS, HEAD_DIM
    )
    key_rows = rotate(key_f, cosine, sine).astype(jnp.bfloat16)
    value_rows = (
        jnp.dot(normed, full_value, preferred_element_type=jnp.float32)
        .astype(jnp.bfloat16)
        .reshape(seq_count, tok_count, KV_HEADS, HEAD_DIM)
    )
    stat_shape = (seq_count, KV_HEADS, group_size, tok_count)
    running_max = jnp.full(stat_shape, masked_value, jnp.float32)
    key_part = lax.all_gather(key_rows, "ctx", axis=1, tiled=True)
    value_part = lax.all_gather(value_rows, "ctx", axis=1, tiled=True)
    key_pos = slot_positions(block_of_slot, jnp.int32(0), key_part.shape[1], half_len)
    visible = query_pos[:, None] >= key_pos[None, :]
    scores = (
        jnp.einsum("sqkgd,snkd->skgqn", queries, key_part, preferred_element_type=jnp.float32)
        * score_scale
    )
    scores = jnp.where(visible, scores, masked_value)
    new_max = jnp.maximum(running_max, jnp.max(scores, axis=-1))
    weights = jnp.where(visible, jnp.exp(scores - new_max[..., None]), 0.0)
    totals = jnp.sum(weights, axis=-1)
    weighted_sum = jnp.einsum(
        "skgqn,snkd->skgqd",
        weights.astype(jnp.bfloat16),
        value_part,
        preferred_element_type=jnp.float32,
    )
    running_max, totals, weighted_sum = (new_max, totals, weighted_sum)
    log_total = running_max + jnp.log(totals)
    attended_f = weighted_sum / totals[..., None]
    attended = (
        attended_f.transpose(0, 3, 1, 2, 4).reshape(rows_all, model_width).astype(jnp.bfloat16)
    )
    hidden_state = inputs + jnp.dot(attended, full_out, preferred_element_type=jnp.float32)
    normed_two_f, scaled_two, inverse_two = norm_forward(hidden_state, gain_mlp_f)
    normed_two = normed_two_f.astype(jnp.bfloat16)
    gate_vals = jnp.dot(normed_two, full_gate, preferred_element_type=jnp.float32)
    up_vals = jnp.dot(normed_two, full_up, preferred_element_type=jnp.float32)
    sigmoid_gate = jax.nn.sigmoid(gate_vals)
    activated = gate_vals * sigmoid_gate
    inner_rows = (activated * up_vals).astype(jnp.bfloat16)
    result = hidden_state + jnp.dot(inner_rows, full_down, preferred_element_type=jnp.float32)
    y_out = result.reshape(seq_count, tok_count, model_width).astype(jnp.bfloat16)
    grad_top = out_grad.reshape(rows_all, model_width)
    grad_residual = grad_top.astype(jnp.float32)
    grad_wdown = jnp.einsum("rf,rd->fd", inner_rows, grad_top, preferred_element_type=jnp.float32)
    grad_inner = jnp.einsum("rd,fd->rf", grad_top, full_down, preferred_element_type=jnp.float32)
    grad_gate = (
        grad_inner * up_vals * sigmoid_gate * (1.0 + gate_vals * (1.0 - sigmoid_gate))
    ).astype(jnp.bfloat16)
    grad_up = (grad_inner * activated).astype(jnp.bfloat16)
    grad_wgate = jnp.einsum("rd,rf->df", normed_two, grad_gate, preferred_element_type=jnp.float32)
    grad_wup = jnp.einsum("rd,rf->df", normed_two, grad_up, preferred_element_type=jnp.float32)
    grad_normed_two = jnp.einsum(
        "rf,df->rd", grad_gate, full_gate, preferred_element_type=jnp.float32
    ) + jnp.einsum("rf,df->rd", grad_up, full_up, preferred_element_type=jnp.float32)
    grad_hidden_norm, grad_gain_mlp = norm_backward(
        grad_normed_two, gain_mlp_f, scaled_two, inverse_two
    )
    grad_hidden = grad_residual + grad_hidden_norm
    grad_branch = grad_hidden.astype(jnp.bfloat16)
    grad_wout = jnp.einsum("ri,rj->ij", attended, grad_branch, preferred_element_type=jnp.float32)
    grad_attended = jnp.einsum(
        "rj,ij->ri", grad_branch, full_out, preferred_element_type=jnp.float32
    ).astype(jnp.bfloat16)
    grad_heads = grad_attended.reshape(
        seq_count, tok_count, KV_HEADS, group_size, HEAD_DIM
    ).transpose(0, 2, 3, 1, 4)
    row_delta = jnp.sum(grad_heads.astype(jnp.float32) * attended_f, axis=-1)

    def block_grads(key_part, value_part, offset):
        key_pos = slot_positions(block_of_slot, offset, key_part.shape[1], half_len)
        visible = query_pos[:, None] >= key_pos[None, :]
        scores = (
            jnp.einsum("sqkgd,snkd->skgqn", queries, key_part, preferred_element_type=jnp.float32)
            * score_scale
        )
        weights = jnp.where(visible, jnp.exp(scores - log_total[..., None]), 0.0)
        grad_value_part = jnp.einsum(
            "skgqn,skgqd->snkd",
            weights.astype(jnp.bfloat16),
            grad_heads,
            preferred_element_type=jnp.float32,
        )
        grad_weights = jnp.einsum(
            "skgqd,snkd->skgqn", grad_heads, value_part, preferred_element_type=jnp.float32
        )
        grad_scores = (weights * (grad_weights - row_delta[..., None])).astype(jnp.bfloat16)
        grad_query_part = jnp.einsum(
            "skgqn,snkd->skgqd", grad_scores, key_part, preferred_element_type=jnp.float32
        )
        grad_key_part = (
            jnp.einsum(
                "skgqn,sqkgd->snkd", grad_scores, queries, preferred_element_type=jnp.float32
            )
            * score_scale
        )
        return (grad_query_part, grad_key_part, grad_value_part)

    grad_query_init = jnp.zeros(stat_shape + (HEAD_DIM,), jnp.float32)
    kv_zero = jnp.zeros(key_rows.shape, jnp.float32)

    def one_hop(hop_index, loop_state):
        key_part, value_part, grad_query, grad_key, grad_value = loop_state
        source = (lax.axis_index("ctx") - hop_index) % ctx_count
        grad_query_part, grad_key_part, grad_value_part = block_grads(
            key_part, value_part, source * tok_count
        )
        key_part, value_part = shifted((key_part, value_part), "ctx", 1)
        grad_key, grad_value = (
            shifted((grad_key + grad_key_part).astype(jnp.bfloat16), "ctx", 1).astype(jnp.float32),
            shifted((grad_value + grad_value_part).astype(jnp.bfloat16), "ctx", 1).astype(
                jnp.float32
            ),
        )
        return (key_part, value_part, grad_query + grad_query_part, grad_key, grad_value)

    loop_state = lax.fori_loop(
        0, ctx_count - 1, one_hop, (key_rows, value_rows, grad_query_init, kv_zero, kv_zero)
    )
    key_part, value_part, grad_query, grad_key, grad_value = loop_state
    source = (lax.axis_index("ctx") + 1) % ctx_count
    grad_query_part, grad_key_part, grad_value_part = block_grads(
        key_part, value_part, source * tok_count
    )
    grad_query = grad_query + grad_query_part
    grad_key, grad_value = (
        shifted((grad_key + grad_key_part).astype(jnp.bfloat16), "ctx", 1).astype(jnp.float32),
        shifted((grad_value + grad_value_part).astype(jnp.bfloat16), "ctx", 1).astype(jnp.float32),
    )
    grad_query_rows = (
        (grad_query * score_scale)
        .transpose(0, 3, 1, 2, 4)
        .reshape(seq_count, tok_count, HEADS, HEAD_DIM)
    )
    grad_query_low = (
        rotate_back(grad_query_rows, cosine, sine)
        .astype(jnp.bfloat16)
        .reshape(rows_all, model_width)
    )
    grad_key_low = (
        rotate_back(grad_key, cosine, sine)
        .astype(jnp.bfloat16)
        .reshape(rows_all, KV_HEADS * HEAD_DIM)
    )
    grad_value_low = grad_value.astype(jnp.bfloat16).reshape(rows_all, KV_HEADS * HEAD_DIM)
    grad_wquery = jnp.einsum(
        "rd,re->de", normed, grad_query_low, preferred_element_type=jnp.float32
    )
    grad_wkey = jnp.einsum("rd,re->de", normed, grad_key_low, preferred_element_type=jnp.float32)
    grad_wvalue = jnp.einsum(
        "rd,re->de", normed, grad_value_low, preferred_element_type=jnp.float32
    )
    grad_normed = jnp.einsum(
        "re,de->rd", grad_query_low, full_query, preferred_element_type=jnp.float32
    )
    grad_normed = grad_normed + jnp.einsum(
        "re,de->rd", grad_key_low, full_key, preferred_element_type=jnp.float32
    )
    grad_normed = grad_normed + jnp.einsum(
        "re,de->rd", grad_value_low, full_value, preferred_element_type=jnp.float32
    )
    grad_input_norm, grad_gain_attn = norm_backward(
        grad_normed, gain_attn_f, scaled_one, inverse_one
    )
    x_grad = (
        (grad_hidden + grad_input_norm)
        .astype(jnp.bfloat16)
        .reshape(seq_count, tok_count, model_width)
    )
    owned_grads = (
        lax.psum_scatter(
            grad_wquery.astype(jnp.bfloat16), "fsdp", scatter_dimension=0, tiled=True
        ).astype(jnp.float32),
        lax.psum_scatter(
            grad_wkey.astype(jnp.bfloat16), "fsdp", scatter_dimension=0, tiled=True
        ).astype(jnp.float32),
        lax.psum_scatter(
            grad_wvalue.astype(jnp.bfloat16), "fsdp", scatter_dimension=0, tiled=True
        ).astype(jnp.float32),
        lax.psum_scatter(
            grad_wout.astype(jnp.bfloat16), "fsdp", scatter_dimension=0, tiled=True
        ).astype(jnp.float32),
        lax.psum_scatter(
            grad_gain_attn.astype(jnp.bfloat16), "fsdp", scatter_dimension=0, tiled=True
        ).astype(jnp.float32),
        lax.psum_scatter(
            grad_wgate.astype(jnp.bfloat16), "fsdp", scatter_dimension=0, tiled=True
        ).astype(jnp.float32),
        lax.psum_scatter(
            grad_wup.astype(jnp.bfloat16), "fsdp", scatter_dimension=0, tiled=True
        ).astype(jnp.float32),
        lax.psum_scatter(
            grad_wdown.astype(jnp.bfloat16), "fsdp", scatter_dimension=0, tiled=True
        ).astype(jnp.float32),
        lax.psum_scatter(
            grad_gain_mlp.astype(jnp.bfloat16), "fsdp", scatter_dimension=0, tiled=True
        ).astype(jnp.float32),
    )
    summed_grads = (
        lax.psum(owned_grads[0].astype(jnp.bfloat16), "ctx").astype(jnp.float32),
        lax.psum(owned_grads[1].astype(jnp.bfloat16), "ctx").astype(jnp.float32),
        lax.psum(owned_grads[2].astype(jnp.bfloat16), "ctx").astype(jnp.float32),
        lax.psum(owned_grads[3].astype(jnp.bfloat16), "ctx").astype(jnp.float32),
        lax.psum(owned_grads[4].astype(jnp.bfloat16), "ctx").astype(jnp.float32),
        lax.psum(owned_grads[5].astype(jnp.bfloat16), "ctx").astype(jnp.float32),
        lax.psum(owned_grads[6].astype(jnp.bfloat16), "ctx").astype(jnp.float32),
        lax.psum(owned_grads[7].astype(jnp.bfloat16), "ctx").astype(jnp.float32),
        lax.psum(owned_grads[8].astype(jnp.bfloat16), "ctx").astype(jnp.float32),
    )
    return (
        y_out,
        x_grad,
        summed_grads[0],
        summed_grads[1],
        summed_grads[2],
        summed_grads[3],
        summed_grads[4],
        summed_grads[5],
        summed_grads[6],
        summed_grads[7],
        summed_grads[8],
    )


def solution(mesh):
    placed = (
        P("fsdp", "ctx", None),
        P("fsdp", None),
        P("fsdp", None),
        P("fsdp", None),
        P("fsdp", None),
        P("fsdp"),
        P("fsdp", None),
        P("fsdp", None),
        P("fsdp", None),
        P("fsdp"),
        P(),
        P("fsdp", "ctx", None),
    )
    return jax.shard_map(
        local,
        mesh=mesh,
        in_specs=placed,
        out_specs=(
            P("fsdp", "ctx", None),
            P("fsdp", "ctx", None),
            P("fsdp", None),
            P("fsdp", None),
            P("fsdp", None),
            P("fsdp", None),
            P("fsdp"),
            P("fsdp", None),
            P("fsdp", None),
            P("fsdp", None),
            P("fsdp"),
        ),
        check_vma=False,
    )
```

profile of v0, /device:TPU:0, one launch (start us, length us, event | category | flops | bytes accessed | tf_op | source)
XLA Modules:
  0.0 655.3 jit_solution(17104645423890764450)
XLA Ops:
  12.6 2.6 all-reduce.7
  15.5 2.0 all_gather.34
  18.4 54.9 %all_gather.35 = bf16[2,1024,3,64]{3,0,2,1:T(2,128)(2,1)} all-gather(bf16[2,64,3,64]{3,0,2,1:T(2,128)(2,1)S(1)} %copy.115), channel_id=1, replica_groups=mesh['ctx'=16,'fsdp'=2] {'ctx'}, dimensions={1}, use_global_device_ids=true | all-gather | bytes 835584 | tf_op jit(solution)/shard_map/all_gather | solution.py:149
  73.3 2.3 all_gather.36
  78.7 3.1 fusion.17
  81.9 2.0 all_gather.37
  84.5 49.6 %all_gather.38 = bf16[2,1024,3,64]{3,0,2,1:T(2,128)(2,1)S(1)} all-gather(bf16[2,64,3,64]{3,0,2,1:T(2,128)(2,1)S(1)} %copy.121), channel_id=1, replica_groups=mesh['ctx'=16,'fsdp'=2] {'ctx'}, dimensions={1}, use_global_device_ids=true | all-gather | bytes 835584 | tf_op jit(solution)/shard_map/all_gather | solution.py:150
  134.2 3.9 fusion.18
  138.1 2.5 fusion.41
  141.1 2.5 all_gather.39
  146.6 1.3 broadcast_compare_fusion.2
  148.8 2.9 fusion.74
  151.7 2.9 fusion.75
  154.5 3.5 multiply_convert_fusion
  163.3 216.1 %while.25 = (s32[]{:T(128)}, bf16[2,64,3,64]{3,1,2,0:T(8,128)(2,1)S(1)}, bf16[2,64,3,64]{3,1,2,0:T(8,128)(2,1)S(1)}, f32[2,3,3,64,64]{4,3,2,1,0:T(8,128)S(1)}, f...) while((s32[]{:T(128)}, ...), condition=%wide.region_10.11_spmd.clone, body=%wide.region_8.10_spmd.clone.sunk | while | flops 48082768 | bytes 4246918 | solution.py:257
  168.7 8.0 %collective-permute-done.2 = bf16[2,64,3,64]{3,1,2,0:T(8,128)(2,1)S(1)} collective-permute-done((bf16[2,64,3,64]{3,1,2,0:T(8,128)(2,1)S(1)}, bf16[2,64,3,64]{3,1,2,0:T(8,128)(2,1)S(1)}, u32[]{:S(2)}, u32[]{:S(2)}) %collective-permute-start.2) | collective-permute-done | bytes 49184 | tf_op jit(solution)/shard_map/while/body/eval_jaxpr/ppermute | solution.py:17
  176.7 1.4 collective-permute-done.3
  182.3 8.6 %collective-permute-done.2 = bf16[2,64,3,64]{3,1,2,0:T(8,128)(2,1)S(1)} collective-permute-done((bf16[2,64,3,64]{3,1,2,0:T(8,128)(2,1)S(1)}, bf16[2,64,3,64]{3,1,2,0:T(8,128)(2,1)S(1)}, u32[]{:S(2)}, u32[]{:S(2)}) %collective-permute-start.2) | collective-permute-done | bytes 49184 | tf_op jit(solution)/shard_map/while/body/eval_jaxpr/ppermute | solution.py:17
  190.9 1.3 collective-permute-done.3
  196.1 2.8 collective-permute-start.3
  199.3 5.9 collective-permute-done.2
  206.5 1.6 collective-permute-start.1
  211.7 2.2 collective-permute-start.3
  214.3 5.3 collective-permute-done.2
  225.8 2.1 collective-permute-start.3
  228.3 5.3 collective-permute-done.2
  238.9 4.3 collective-permute-start.3
  243.6 3.4 collective-permute-done.2
  248.3 3.4 collective-permute-start.1
  255.6 2.3 collective-permute-start.3
  258.3 4.9 collective-permute-done.2
  269.1 1.8 collective-permute-start.3
  271.3 5.8 collective-permute-done.2
  277.0 1.8 collective-permute-done.3
  283.1 2.1 collective-permute-start.3
  285.5 6.4 collective-permute-done.2
  292.0 1.9 collective-permute-done.3
  297.7 3.1 collective-permute-start.3
  301.2 6.1 collective-permute-done.2
  307.3 2.1 collective-permute-done.3
  314.8 8.1 %collective-permute-done.2 = bf16[2,64,3,64]{3,1,2,0:T(8,128)(2,1)S(1)} collective-permute-done((bf16[2,64,3,64]{3,1,2,0:T(8,128)(2,1)S(1)}, bf16[2,64,3,64]{3,1,2,0:T(8,128)(2,1)S(1)}, u32[]{:S(2)}, u32[]{:S(2)}) %collective-permute-start.2) | collective-permute-done | bytes 49184 | tf_op jit(solution)/shard_map/while/body/eval_jaxpr/ppermute | solution.py:17
  322.9 1.3 collective-permute-done.3
  328.5 8.6 %collective-permute-done.2 = bf16[2,64,3,64]{3,1,2,0:T(8,128)(2,1)S(1)} collective-permute-done((bf16[2,64,3,64]{3,1,2,0:T(8,128)(2,1)S(1)}, bf16[2,64,3,64]{3,1,2,0:T(8,128)(2,1)S(1)}, u32[]{:S(2)}, u32[]{:S(2)}) %collective-permute-start.2) | collective-permute-done | bytes 49184 | tf_op jit(solution)/shard_map/while/body/eval_jaxpr/ppermute | solution.py:17
  342.2 2.0 collective-permute-start.3
  344.6 6.6 %collective-permute-done.2 = bf16[2,64,3,64]{3,1,2,0:T(8,128)(2,1)S(1)} collective-permute-done((bf16[2,64,3,64]{3,1,2,0:T(8,128)(2,1)S(1)}, bf16[2,64,3,64]{3,1,2,0:T(8,128)(2,1)S(1)}, u32[]{:S(2)}, u32[]{:S(2)}) %collective-permute-start.2) | collective-permute-done | bytes 49184 | tf_op jit(solution)/shard_map/while/body/eval_jaxpr/ppermute | solution.py:17
  357.6 7.6 %collective-permute-done.2 = bf16[2,64,3,64]{3,1,2,0:T(8,128)(2,1)S(1)} collective-permute-done((bf16[2,64,3,64]{3,1,2,0:T(8,128)(2,1)S(1)}, bf16[2,64,3,64]{3,1,2,0:T(8,128)(2,1)S(1)}, u32[]{:S(2)}, u32[]{:S(2)}) %collective-permute-start.2) | collective-permute-done | bytes 49184 | tf_op jit(solution)/shard_map/while/body/eval_jaxpr/ppermute | solution.py:17
  370.4 2.6 collective-permute-start.3
  373.3 5.0 collective-permute-done.2
  381.8 7.3 %collective-permute-done.5 = bf16[2,64,3,64]{1,3,2,0:T(8,128)(2,1)S(1)} collective-permute-done((bf16[2,64,3,64]{1,3,2,0:T(8,128)(2,1)S(1)}, bf16[2,64,3,64]{1,3,2,0:T(8,128)(2,1)S(1)}, u32[]{:S(2)}, u32[]{:S(2)}) %collective-permute-start.5) | collective-permute-done | bytes 49184 | tf_op jit(solution)/shard_map/ppermute | solution.py:17
  395.6 1.8 convolution_convert_fusion.1
  397.5 1.8 convolution_convert_fusion.2
  399.4 1.9 convolution_convert_fusion
  401.6 3.7 reduce-scatter.10.cloned.1.call-done
  405.3 11.5 %reduce-scatter.14.cloned.1.call-done = bf16[288,576]{1,0:T(8,128)(2,1)} async-done(((bf16[576,576]{1,0:T(8,128)(2,1)}), bf16[288,576]{1,0:T(8,128)(2,1)}) %reduce-scatter.14.cloned.1.call-update) | async-done | bytes 331792 | tf_op jit(solution)/shard_map/reduce_scatter | solution.py:320
  416.8 12.2 %reduce-scatter.8.cloned.1.call-done = bf16[288,576]{1,0:T(8,128)(2,1)} async-done(((bf16[576,576]{1,0:T(8,128)(2,1)}), bf16[288,576]{1,0:T(8,128)(2,1)}) %reduce-scatter.8.cloned.1.call-update) | async-done | bytes 331792 | tf_op jit(solution)/shard_map/reduce_scatter | solution.py:311
  429.0 13.3 %reduce-scatter.18.cloned.1.call-done = bf16[288,1536]{1,0:T(8,128)(2,1)} async-done(((bf16[576,1536]{1,0:T(8,128)(2,1)}), bf16[288,1536]{1,0:T(8,128)(2,1)}) %reduce-scatter.18.cloned.1.call-update) | async-done | bytes 884752 | tf_op jit(solution)/shard_map/reduce_scatter | solution.py:329
  442.4 13.4 %reduce-scatter.16.cloned.1.call-done = bf16[288,1536]{1,0:T(8,128)(2,1)} async-done(((bf16[576,1536]{1,0:T(8,128)(2,1)}), bf16[288,1536]{1,0:T(8,128)(2,1)}) %reduce-scatter.16.cloned.1.call-update) | async-done | bytes 884752 | tf_op jit(solution)/shard_map/reduce_scatter | solution.py:326
  455.8 13.2 %reduce-scatter.20.cloned.1.call-done = bf16[768,576]{0,1:T(8,128)(2,1)} async-done(((bf16[1536,576]{0,1:T(8,128)(2,1)}), bf16[768,576]{0,1:T(8,128)(2,1)}) %reduce-scatter.20.cloned.1.call-update) | async-done | bytes 884752 | tf_op jit(solution)/shard_map/reduce_scatter | solution.py:332
  469.7 2.1 fusion.33
  473.7 2.5 all-reduce.6
  476.4 43.7 %all-reduce.4 = (bf16[288]{0:T(512)(128)(2,1)S(1)}, bf16[288]{0:T(512)(128)(2,1)S(1)}) all-reduce(bf16[288]{0:T(512)(128)(2,1)S(1)} %dynamic-slice.3, bf16[288]{0:T(512)(128)(2,1)S(1)} %dynamic-slice.5), channel_id=1, replica_groups=mesh['ctx'=16,'fsdp'=2] {'ctx'}, use_global_device_ids=true, to_apply=%region_23.24 | all-reduce | flops 576 | bytes 2304 | tf_op jit(solution)/shard_map/psum | solution.py:344
  522.2 117.8 %all-reduce.10.cloned.1.call-done = (bf16[288,576]{1,0:T(8,128)(2,1)}, bf16[288,192]{1,0:T(8,128)(2,1)}, bf16[288,192]{1,0:T(8,128)(2,1)}, bf16[288,576]{1,0:T(8...) async-done(((bf16[288,576]{1,0:T(8,128)(2,1)}, bf16[288,192]{1,0:T(8,128)(2,1)}, bf16[288,192]{1,0:T(8,128)(2,1)}, ...) | async-done | bytes 3538960 | tf_op jit(solution)/shard_map/psum | solution.py:340
  640.0 2.7 convert_element_type.301
  642.7 1.4 convert_element_type.303
  (509 shorter events, 114.7 us)
Async XLA Ops:
  7.2 141.5 %all-gather.4.cloned.1.call-start = ((), (), s32[]{:S(2)}) async-start(), calls=%async_computation.7 | async-start | bytes 2654208 | tf_op jit(solution)/shard_map/all_gather | solution.py:100
  8.0 143.7 %all-gather.6.cloned.1.call-start = ((), (), s32[]{:S(2)}) async-start(), calls=%async_computation.8 | async-start | bytes 2654208 | tf_op jit(solution)/shard_map/all_gather | solution.py:101
  8.7 145.8 %all-gather.8.cloned.1.call-start = ((), (), s32[]{:S(2)}) async-start(), calls=%async_computation.9 | async-start | bytes 2654208 | tf_op jit(solution)/shard_map/all_gather | solution.py:102
  9.4 392.2 %reduce-scatter.12.cloned.1.call-start = ((), (), s32[]{:S(2)}) async-start(), calls=%async_computation.12 | async-start | bytes 442368 | tf_op jit(solution)/shard_map/reduce_scatter | solution.py:317
  163.3 14.8 %collective-permute-start = (bf16[2,64,3,64]{3,1,2,0:T(8,128)(2,1)S(1)}, bf16[2,64,3,64]{3,1,2,0:T(8,128)(2,1)S(1)}, u32[]{:S(2)}, u32[]{:S(2)}) collective-permute-start(bf16[2,64,3,64]{3,1,2,0:T(8,128)(2,1)S(1)} %copy.200), channel_id=1, source_target_pairs={{30,0},{0,2},{2,4},{4,6},{6,8},{8,10},{10,12},{12,14},{14,16},{16,... | collective-permute-start | bytes 147464 | tf_op jit(solution)/shard_map/while/body/eval_jaxpr/ppermute | solution.py:17
  164.0 14.1 %collective-permute-start.1 = (bf16[2,64,3,64]{3,1,2,0:T(8,128)(2,1)S(1)}, bf16[2,64,3,64]{3,1,2,0:T(8,128)(2,1)S(1)}, u32[]{:S(2)}, u32[]{:S(2)}) collective-permute-start(bf16[2,64,3,64]{3,1,2,0:T(8,128)(2,1)S(1)} %copy.201), channel_id=1, source_target_pairs={{30,0},{0,2},{2,4},{4,6},{6,8},{8,10},{10,12},{12,14},{14,16},{16,... | collective-permute-start | bytes 147464 | tf_op jit(solution)/shard_map/while/body/eval_jaxpr/ppermute | solution.py:17
  167.3 9.3 %collective-permute-start.2 = (bf16[2,64,3,64]{3,1,2,0:T(8,128)(2,1)S(1)}, bf16[2,64,3,64]{3,1,2,0:T(8,128)(2,1)S(1)}, u32[]{:S(2)}, u32[]{:S(2)}) collective-permute-start(bf16[2,64,3,64]{3,1,2,0:T(8,128)(2,1)S(1)} %fusion.154), channel_id=1, source_target_pairs={{30,0},{0,2},{2,4},{4,6},{6,8},{8,10},{10,12},{12,14},{14,16},{16,... | collective-permute-start | bytes 147464 | tf_op jit(solution)/shard_map/while/body/eval_jaxpr/ppermute | solution.py:17
  167.7 10.4 %collective-permute-start.3 = (bf16[2,64,3,64]{3,1,2,0:T(8,128)(2,1)S(1)}, bf16[2,64,3,64]{3,1,2,0:T(8,128)(2,1)S(1)}, u32[]{:S(2)}, u32[]{:S(2)}) collective-permute-start(bf16[2,64,3,64]{3,1,2,0:T(8,128)(2,1)S(1)} %fusion.155), channel_id=1, source_target_pairs={{30,0},{0,2},{2,4},{4,6},{6,8},{8,10},{10,12},{12,14},{14,16},{16,... | collective-permute-start | bytes 147464 | tf_op jit(solution)/shard_map/while/body/eval_jaxpr/ppermute | solution.py:17
  178.2 14.1 %collective-permute-start = (bf16[2,64,3,64]{3,1,2,0:T(8,128)(2,1)S(1)}, bf16[2,64,3,64]{3,1,2,0:T(8,128)(2,1)S(1)}, u32[]{:S(2)}, u32[]{:S(2)}) collective-permute-start(bf16[2,64,3,64]{3,1,2,0:T(8,128)(2,1)S(1)} %copy.200), channel_id=1, source_target_pairs={{30,0},{0,2},{2,4},{4,6},{6,8},{8,10},{10,12},{12,14},{14,16},{16,... | collective-permute-start | bytes 147464 | tf_op jit(solution)/shard_map/while/body/eval_jaxpr/ppermute | solution.py:17
  178.2 14.1 %collective-permute-start.1 = (bf16[2,64,3,64]{3,1,2,0:T(8,128)(2,1)S(1)}, bf16[2,64,3,64]{3,1,2,0:T(8,128)(2,1)S(1)}, u32[]{:S(2)}, u32[]{:S(2)}) collective-permute-start(bf16[2,64,3,64]{3,1,2,0:T(8,128)(2,1)S(1)} %copy.201), channel_id=1, source_target_pairs={{30,0},{0,2},{2,4},{4,6},{6,8},{8,10},{10,12},{12,14},{14,16},{16,... | collective-permute-start | bytes 147464 | tf_op jit(solution)/shard_map/while/body/eval_jaxpr/ppermute | solution.py:17
  181.6 9.3 %collective-permute-start.2 = (bf16[2,64,3,64]{3,1,2,0:T(8,128)(2,1)S(1)}, bf16[2,64,3,64]{3,1,2,0:T(8,128)(2,1)S(1)}, u32[]{:S(2)}, u32[]{:S(2)}) collective-permute-start(bf16[2,64,3,64]{3,1,2,0:T(8,128)(2,1)S(1)} %fusion.154), channel_id=1, source_target_pairs={{30,0},{0,2},{2,4},{4,6},{6,8},{8,10},{10,12},{12,14},{14,16},{16,... | collective-permute-start | bytes 147464 | tf_op jit(solution)/shard_map/while/body/eval_jaxpr/ppermute | solution.py:17
  181.9 10.4 %collective-permute-start.3 = (bf16[2,64,3,64]{3,1,2,0:T(8,128)(2,1)S(1)}, bf16[2,64,3,64]{3,1,2,0:T(8,128)(2,1)S(1)}, u32[]{:S(2)}, u32[]{:S(2)}) collective-permute-start(bf16[2,64,3,64]{3,1,2,0:T(8,128)(2,1)S(1)} %fusion.155), channel_id=1, source_target_pairs={{30,0},{0,2},{2,4},{4,6},{6,8},{8,10},{10,12},{12,14},{14,16},{16,... | collective-permute-start | bytes 147464 | tf_op jit(solution)/shard_map/while/body/eval_jaxpr/ppermute | solution.py:17
  192.4 14.1 %collective-permute-start = (bf16[2,64,3,64]{3,1,2,0:T(8,128)(2,1)S(1)}, bf16[2,64,3,64]{3,1,2,0:T(8,128)(2,1)S(1)}, u32[]{:S(2)}, u32[]{:S(2)}) collective-permute-start(bf16[2,64,3,64]{3,1,2,0:T(8,128)(2,1)S(1)} %copy.200), channel_id=1, source_target_pairs={{30,0},{0,2},{2,4},{4,6},{6,8},{8,10},{10,12},{12,14},{14,16},{16,... | collective-permute-start | bytes 147464 | tf_op jit(solution)/shard_map/while/body/eval_jaxpr/ppermute | solution.py:17
  192.4 14.0 %collective-permute-start.1 = (bf16[2,64,3,64]{3,1,2,0:T(8,128)(2,1)S(1)}, bf16[2,64,3,64]{3,1,2,0:T(8,128)(2,1)S(1)}, u32[]{:S(2)}, u32[]{:S(2)}) collective-permute-start(bf16[2,64,3,64]{3,1,2,0:T(8,128)(2,1)S(1)} %copy.201), channel_id=1, source_target_pairs={{30,0},{0,2},{2,4},{4,6},{6,8},{8,10},{10,12},{12,14},{14,16},{16,... | collective-permute-start | bytes 147464 | tf_op jit(solution)/shard_map/while/body/eval_jaxpr/ppermute | solution.py:17
  195.8 9.4 %collective-permute-start.2 = (bf16[2,64,3,64]{3,1,2,0:T(8,128)(2,1)S(1)}, bf16[2,64,3,64]{3,1,2,0:T(8,128)(2,1)S(1)}, u32[]{:S(2)}, u32[]{:S(2)}) collective-permute-start(bf16[2,64,3,64]{3,1,2,0:T(8,128)(2,1)S(1)} %fusion.154), channel_id=1, source_target_pairs={{30,0},{0,2},{2,4},{4,6},{6,8},{8,10},{10,12},{12,14},{14,16},{16,... | collective-permute-start | bytes 147464 | tf_op jit(solution)/shard_map/while/body/eval_jaxpr/ppermute | solution.py:17
  196.1 10.3 %collective-permute-start.3 = (bf16[2,64,3,64]{3,1,2,0:T(8,128)(2,1)S(1)}, bf16[2,64,3,64]{3,1,2,0:T(8,128)(2,1)S(1)}, u32[]{:S(2)}, u32[]{:S(2)}) collective-permute-start(bf16[2,64,3,64]{3,1,2,0:T(8,128)(2,1)S(1)} %fusion.155), channel_id=1, source_target_pairs={{30,0},{0,2},{2,4},{4,6},{6,8},{8,10},{10,12},{12,14},{14,16},{16,... | collective-permute-start | bytes 147464 | tf_op jit(solution)/shard_map/while/body/eval_jaxpr/ppermute | solution.py:17
  206.5 14.2 %collective-permute-start = (bf16[2,64,3,64]{3,1,2,0:T(8,128)(2,1)S(1)}, bf16[2,64,3,64]{3,1,2,0:T(8,128)(2,1)S(1)}, u32[]{:S(2)}, u32[]{:S(2)}) collective-permute-start(bf16[2,64,3,64]{3,1,2,0:T(8,128)(2,1)S(1)} %copy.200), channel_id=1, source_target_pairs={{30,0},{0,2},{2,4},{4,6},{6,8},{8,10},{10,12},{12,14},{14,16},{16,... | collective-permute-start | bytes 147464 | tf_op jit(solution)/shard_map/while/body/eval_jaxpr/ppermute | solution.py:17
  206.5 14.2 %collective-permute-start.1 = (bf16[2,64,3,64]{3,1,2,0:T(8,128)(2,1)S(1)}, bf16[2,64,3,64]{3,1,2,0:T(8,128)(2,1)S(1)}, u32[]{:S(2)}, u32[]{:S(2)}) collective-permute-start(bf16[2,64,3,64]{3,1,2,0:T(8,128)(2,1)S(1)} %copy.201), channel_id=1, source_target_pairs={{30,0},{0,2},{2,4},{4,6},{6,8},{8,10},{10,12},{12,14},{14,16},{16,... | collective-permute-start | bytes 147464 | tf_op jit(solution)/shard_map/while/body/eval_jaxpr/ppermute | solution.py:17
  211.7 8.9 %collective-permute-start.3 = (bf16[2,64,3,64]{3,1,2,0:T(8,128)(2,1)S(1)}, bf16[2,64,3,64]{3,1,2,0:T(8,128)(2,1)S(1)}, u32[]{:S(2)}, u32[]{:S(2)}) collective-permute-start(bf16[2,64,3,64]{3,1,2,0:T(8,128)(2,1)S(1)} %fusion.155), channel_id=1, source_target_pairs={{30,0},{0,2},{2,4},{4,6},{6,8},{8,10},{10,12},{12,14},{14,16},{16,... | collective-permute-start | bytes 147464 | tf_op jit(solution)/shard_map/while/body/eval_jaxpr/ppermute | solution.py:17
  220.8 13.8 %collective-permute-start = (bf16[2,64,3,64]{3,1,2,0:T(8,128)(2,1)S(1)}, bf16[2,64,3,64]{3,1,2,0:T(8,128)(2,1)S(1)}, u32[]{:S(2)}, u32[]{:S(2)}) collective-permute-start(bf16[2,64,3,64]{3,1,2,0:T(8,128)(2,1)S(1)} %copy.200), channel_id=1, source_target_pairs={{30,0},{0,2},{2,4},{4,6},{6,8},{8,10},{10,12},{12,14},{14,16},{16,... | collective-permute-start | bytes 147464 | tf_op jit(solution)/shard_map/while/body/eval_jaxpr/ppermute | solution.py:17
  220.8 13.8 %collective-permute-start.1 = (bf16[2,64,3,64]{3,1,2,0:T(8,128)(2,1)S(1)}, bf16[2,64,3,64]{3,1,2,0:T(8,128)(2,1)S(1)}, u32[]{:S(2)}, u32[]{:S(2)}) collective-permute-start(bf16[2,64,3,64]{3,1,2,0:T(8,128)(2,1)S(1)} %copy.201), channel_id=1, source_target_pairs={{30,0},{0,2},{2,4},{4,6},{6,8},{8,10},{10,12},{12,14},{14,16},{16,... | collective-permute-start | bytes 147464 | tf_op jit(solution)/shard_map/while/body/eval_jaxpr/ppermute | solution.py:17
  225.8 8.8 %collective-permute-start.3 = (bf16[2,64,3,64]{3,1,2,0:T(8,128)(2,1)S(1)}, bf16[2,64,3,64]{3,1,2,0:T(8,128)(2,1)S(1)}, u32[]{:S(2)}, u32[]{:S(2)}) collective-permute-start(bf16[2,64,3,64]{3,1,2,0:T(8,128)(2,1)S(1)} %fusion.155), channel_id=1, source_target_pairs={{30,0},{0,2},{2,4},{4,6},{6,8},{8,10},{10,12},{12,14},{14,16},{16,... | collective-permute-start | bytes 147464 | tf_op jit(solution)/shard_map/while/body/eval_jaxpr/ppermute | solution.py:17
  234.7 13.4 %collective-permute-start = (bf16[2,64,3,64]{3,1,2,0:T(8,128)(2,1)S(1)}, bf16[2,64,3,64]{3,1,2,0:T(8,128)(2,1)S(1)}, u32[]{:S(2)}, u32[]{:S(2)}) collective-permute-start(bf16[2,64,3,64]{3,1,2,0:T(8,128)(2,1)S(1)} %copy.200), channel_id=1, source_target_pairs={{30,0},{0,2},{2,4},{4,6},{6,8},{8,10},{10,12},{12,14},{14,16},{16,... | collective-permute-start | bytes 147464 | tf_op jit(solution)/shard_map/while/body/eval_jaxpr/ppermute | solution.py:17
  234.7 13.3 %collective-permute-start.1 = (bf16[2,64,3,64]{3,1,2,0:T(8,128)(2,1)S(1)}, bf16[2,64,3,64]{3,1,2,0:T(8,128)(2,1)S(1)}, u32[]{:S(2)}, u32[]{:S(2)}) collective-permute-start(bf16[2,64,3,64]{3,1,2,0:T(8,128)(2,1)S(1)} %copy.201), channel_id=1, source_target_pairs={{30,0},{0,2},{2,4},{4,6},{6,8},{8,10},{10,12},{12,14},{14,16},{16,... | collective-permute-start | bytes 147464 | tf_op jit(solution)/shard_map/while/body/eval_jaxpr/ppermute | solution.py:17
  238.9 9.2 %collective-permute-start.3 = (bf16[2,64,3,64]{3,1,2,0:T(8,128)(2,1)S(1)}, bf16[2,64,3,64]{3,1,2,0:T(8,128)(2,1)S(1)}, u32[]{:S(2)}, u32[]{:S(2)}) collective-permute-start(bf16[2,64,3,64]{3,1,2,0:T(8,128)(2,1)S(1)} %fusion.155), channel_id=1, source_target_pairs={{30,0},{0,2},{2,4},{4,6},{6,8},{8,10},{10,12},{12,14},{14,16},{16,... | collective-permute-start | bytes 147464 | tf_op jit(solution)/shard_map/while/body/eval_jaxpr/ppermute | solution.py:17
  248.1 16.2 %collective-permute-start = (bf16[2,64,3,64]{3,1,2,0:T(8,128)(2,1)S(1)}, bf16[2,64,3,64]{3,1,2,0:T(8,128)(2,1)S(1)}, u32[]{:S(2)}, u32[]{:S(2)}) collective-permute-start(bf16[2,64,3,64]{3,1,2,0:T(8,128)(2,1)S(1)} %copy.200), channel_id=1, source_target_pairs={{30,0},{0,2},{2,4},{4,6},{6,8},{8,10},{10,12},{12,14},{14,16},{16,... | collective-permute-start | bytes 147464 | tf_op jit(solution)/shard_map/while/body/eval_jaxpr/ppermute | solution.py:17
  248.3 16.0 %collective-permute-start.1 = (bf16[2,64,3,64]{3,1,2,0:T(8,128)(2,1)S(1)}, bf16[2,64,3,64]{3,1,2,0:T(8,128)(2,1)S(1)}, u32[]{:S(2)}, u32[]{:S(2)}) collective-permute-start(bf16[2,64,3,64]{3,1,2,0:T(8,128)(2,1)S(1)} %copy.201), channel_id=1, source_target_pairs={{30,0},{0,2},{2,4},{4,6},{6,8},{8,10},{10,12},{12,14},{14,16},{16,... | collective-permute-start | bytes 147464 | tf_op jit(solution)/shard_map/while/body/eval_jaxpr/ppermute | solution.py:17
  264.3 14.5 %collective-permute-start = (bf16[2,64,3,64]{3,1,2,0:T(8,128)(2,1)S(1)}, bf16[2,64,3,64]{3,1,2,0:T(8,128)(2,1)S(1)}, u32[]{:S(2)}, u32[]{:S(2)}) collective-permute-start(bf16[2,64,3,64]{3,1,2,0:T(8,128)(2,1)S(1)} %copy.200), channel_id=1, source_target_pairs={{30,0},{0,2},{2,4},{4,6},{6,8},{8,10},{10,12},{12,14},{14,16},{16,... | collective-permute-start | bytes 147464 | tf_op jit(solution)/shard_map/while/body/eval_jaxpr/ppermute | solution.py:17
  264.4 14.4 %collective-permute-start.1 = (bf16[2,64,3,64]{3,1,2,0:T(8,128)(2,1)S(1)}, bf16[2,64,3,64]{3,1,2,0:T(8,128)(2,1)S(1)}, u32[]{:S(2)}, u32[]{:S(2)}) collective-permute-start(bf16[2,64,3,64]{3,1,2,0:T(8,128)(2,1)S(1)} %copy.201), channel_id=1, source_target_pairs={{30,0},{0,2},{2,4},{4,6},{6,8},{8,10},{10,12},{12,14},{14,16},{16,... | collective-permute-start | bytes 147464 | tf_op jit(solution)/shard_map/while/body/eval_jaxpr/ppermute | solution.py:17
  269.1 9.7 %collective-permute-start.3 = (bf16[2,64,3,64]{3,1,2,0:T(8,128)(2,1)S(1)}, bf16[2,64,3,64]{3,1,2,0:T(8,128)(2,1)S(1)}, u32[]{:S(2)}, u32[]{:S(2)}) collective-permute-start(bf16[2,64,3,64]{3,1,2,0:T(8,128)(2,1)S(1)} %fusion.155), channel_id=1, source_target_pairs={{30,0},{0,2},{2,4},{4,6},{6,8},{8,10},{10,12},{12,14},{14,16},{16,... | collective-permute-start | bytes 147464 | tf_op jit(solution)/shard_map/while/body/eval_jaxpr/ppermute | solution.py:17
  278.9 15.0 %collective-permute-start = (bf16[2,64,3,64]{3,1,2,0:T(8,128)(2,1)S(1)}, bf16[2,64,3,64]{3,1,2,0:T(8,128)(2,1)S(1)}, u32[]{:S(2)}, u32[]{:S(2)}) collective-permute-start(bf16[2,64,3,64]{3,1,2,0:T(8,128)(2,1)S(1)} %copy.200), channel_id=1, source_target_pairs={{30,0},{0,2},{2,4},{4,6},{6,8},{8,10},{10,12},{12,14},{14,16},{16,... | collective-permute-start | bytes 147464 | tf_op jit(solution)/shard_map/while/body/eval_jaxpr/ppermute | solution.py:17
  279.0 15.0 %collective-permute-start.1 = (bf16[2,64,3,64]{3,1,2,0:T(8,128)(2,1)S(1)}, bf16[2,64,3,64]{3,1,2,0:T(8,128)(2,1)S(1)}, u32[]{:S(2)}, u32[]{:S(2)}) collective-permute-start(bf16[2,64,3,64]{3,1,2,0:T(8,128)(2,1)S(1)} %copy.201), channel_id=1, source_target_pairs={{30,0},{0,2},{2,4},{4,6},{6,8},{8,10},{10,12},{12,14},{14,16},{16,... | collective-permute-start | bytes 147464 | tf_op jit(solution)/shard_map/while/body/eval_jaxpr/ppermute | solution.py:17
  282.7 9.3 %collective-permute-start.2 = (bf16[2,64,3,64]{3,1,2,0:T(8,128)(2,1)S(1)}, bf16[2,64,3,64]{3,1,2,0:T(8,128)(2,1)S(1)}, u32[]{:S(2)}, u32[]{:S(2)}) collective-permute-start(bf16[2,64,3,64]{3,1,2,0:T(8,128)(2,1)S(1)} %fusion.154), channel_id=1, source_target_pairs={{30,0},{0,2},{2,4},{4,6},{6,8},{8,10},{10,12},{12,14},{14,16},{16,... | collective-permute-start | bytes 147464 | tf_op jit(solution)/shard_map/while/body/eval_jaxpr/ppermute | solution.py:17
  283.1 10.8 %collective-permute-start.3 = (bf16[2,64,3,64]{3,1,2,0:T(8,128)(2,1)S(1)}, bf16[2,64,3,64]{3,1,2,0:T(8,128)(2,1)S(1)}, u32[]{:S(2)}, u32[]{:S(2)}) collective-permute-start(bf16[2,64,3,64]{3,1,2,0:T(8,128)(2,1)S(1)} %fusion.155), channel_id=1, source_target_pairs={{30,0},{0,2},{2,4},{4,6},{6,8},{8,10},{10,12},{12,14},{14,16},{16,... | collective-permute-start | bytes 147464 | tf_op jit(solution)/shard_map/while/body/eval_jaxpr/ppermute | solution.py:17
  294.0 15.4 %collective-permute-start = (bf16[2,64,3,64]{3,1,2,0:T(8,128)(2,1)S(1)}, bf16[2,64,3,64]{3,1,2,0:T(8,128)(2,1)S(1)}, u32[]{:S(2)}, u32[]{:S(2)}) collective-permute-start(bf16[2,64,3,64]{3,1,2,0:T(8,128)(2,1)S(1)} %copy.200), channel_id=1, source_target_pairs={{30,0},{0,2},{2,4},{4,6},{6,8},{8,10},{10,12},{12,14},{14,16},{16,... | collective-permute-start | bytes 147464 | tf_op jit(solution)/shard_map/while/body/eval_jaxpr/ppermute | solution.py:17
  294.1 15.4 %collective-permute-start.1 = (bf16[2,64,3,64]{3,1,2,0:T(8,128)(2,1)S(1)}, bf16[2,64,3,64]{3,1,2,0:T(8,128)(2,1)S(1)}, u32[]{:S(2)}, u32[]{:S(2)}) collective-permute-start(bf16[2,64,3,64]{3,1,2,0:T(8,128)(2,1)S(1)} %copy.201), channel_id=1, source_target_pairs={{30,0},{0,2},{2,4},{4,6},{6,8},{8,10},{10,12},{12,14},{14,16},{16,... | collective-permute-start | bytes 147464 | tf_op jit(solution)/shard_map/while/body/eval_jaxpr/ppermute | solution.py:17
  297.4 9.9 %collective-permute-start.2 = (bf16[2,64,3,64]{3,1,2,0:T(8,128)(2,1)S(1)}, bf16[2,64,3,64]{3,1,2,0:T(8,128)(2,1)S(1)}, u32[]{:S(2)}, u32[]{:S(2)}) collective-permute-start(bf16[2,64,3,64]{3,1,2,0:T(8,128)(2,1)S(1)} %fusion.154), channel_id=1, source_target_pairs={{30,0},{0,2},{2,4},{4,6},{6,8},{8,10},{10,12},{12,14},{14,16},{16,... | collective-permute-start | bytes 147464 | tf_op jit(solution)/shard_map/while/body/eval_jaxpr/ppermute | solution.py:17
  297.7 11.7 %collective-permute-start.3 = (bf16[2,64,3,64]{3,1,2,0:T(8,128)(2,1)S(1)}, bf16[2,64,3,64]{3,1,2,0:T(8,128)(2,1)S(1)}, u32[]{:S(2)}, u32[]{:S(2)}) collective-permute-start(bf16[2,64,3,64]{3,1,2,0:T(8,128)(2,1)S(1)} %fusion.155), channel_id=1, source_target_pairs={{30,0},{0,2},{2,4},{4,6},{6,8},{8,10},{10,12},{12,14},{14,16},{16,... | collective-permute-start | bytes 147464 | tf_op jit(solution)/shard_map/while/body/eval_jaxpr/ppermute | solution.py:17
  309.5 14.8 %collective-permute-start = (bf16[2,64,3,64]{3,1,2,0:T(8,128)(2,1)S(1)}, bf16[2,64,3,64]{3,1,2,0:T(8,128)(2,1)S(1)}, u32[]{:S(2)}, u32[]{:S(2)}) collective-permute-start(bf16[2,64,3,64]{3,1,2,0:T(8,128)(2,1)S(1)} %copy.200), channel_id=1, source_target_pairs={{30,0},{0,2},{2,4},{4,6},{6,8},{8,10},{10,12},{12,14},{14,16},{16,... | collective-permute-start | bytes 147464 | tf_op jit(solution)/shard_map/while/body/eval_jaxpr/ppermute | solution.py:17
  309.5 14.7 %collective-permute-start.1 = (bf16[2,64,3,64]{3,1,2,0:T(8,128)(2,1)S(1)}, bf16[2,64,3,64]{3,1,2,0:T(8,128)(2,1)S(1)}, u32[]{:S(2)}, u32[]{:S(2)}) collective-permute-start(bf16[2,64,3,64]{3,1,2,0:T(8,128)(2,1)S(1)} %copy.201), channel_id=1, source_target_pairs={{30,0},{0,2},{2,4},{4,6},{6,8},{8,10},{10,12},{12,14},{14,16},{16,... | collective-permute-start | bytes 147464 | tf_op jit(solution)/shard_map/while/body/eval_jaxpr/ppermute | solution.py:17
  312.9 10.0 %collective-permute-start.2 = (bf16[2,64,3,64]{3,1,2,0:T(8,128)(2,1)S(1)}, bf16[2,64,3,64]{3,1,2,0:T(8,128)(2,1)S(1)}, u32[]{:S(2)}, u32[]{:S(2)}) collective-permute-start(bf16[2,64,3,64]{3,1,2,0:T(8,128)(2,1)S(1)} %fusion.154), channel_id=1, source_target_pairs={{30,0},{0,2},{2,4},{4,6},{6,8},{8,10},{10,12},{12,14},{14,16},{16,... | collective-permute-start | bytes 147464 | tf_op jit(solution)/shard_map/while/body/eval_jaxpr/ppermute | solution.py:17
  313.2 11.0 %collective-permute-start.3 = (bf16[2,64,3,64]{3,1,2,0:T(8,128)(2,1)S(1)}, bf16[2,64,3,64]{3,1,2,0:T(8,128)(2,1)S(1)}, u32[]{:S(2)}, u32[]{:S(2)}) collective-permute-start(bf16[2,64,3,64]{3,1,2,0:T(8,128)(2,1)S(1)} %fusion.155), channel_id=1, source_target_pairs={{30,0},{0,2},{2,4},{4,6},{6,8},{8,10},{10,12},{12,14},{14,16},{16,... | collective-permute-start | bytes 147464 | tf_op jit(solution)/shard_map/while/body/eval_jaxpr/ppermute | solution.py:17
  324.3 14.1 %collective-permute-start = (bf16[2,64,3,64]{3,1,2,0:T(8,128)(2,1)S(1)}, bf16[2,64,3,64]{3,1,2,0:T(8,128)(2,1)S(1)}, u32[]{:S(2)}, u32[]{:S(2)}) collective-permute-start(bf16[2,64,3,64]{3,1,2,0:T(8,128)(2,1)S(1)} %copy.200), channel_id=1, source_target_pairs={{30,0},{0,2},{2,4},{4,6},{6,8},{8,10},{10,12},{12,14},{14,16},{16,... | collective-permute-start | bytes 147464 | tf_op jit(solution)/shard_map/while/body/eval_jaxpr/ppermute | solution.py:17
  324.4 14.0 %collective-permute-start.1 = (bf16[2,64,3,64]{3,1,2,0:T(8,128)(2,1)S(1)}, bf16[2,64,3,64]{3,1,2,0:T(8,128)(2,1)S(1)}, u32[]{:S(2)}, u32[]{:S(2)}) collective-permute-start(bf16[2,64,3,64]{3,1,2,0:T(8,128)(2,1)S(1)} %copy.201), channel_id=1, source_target_pairs={{30,0},{0,2},{2,4},{4,6},{6,8},{8,10},{10,12},{12,14},{14,16},{16,... | collective-permute-start | bytes 147464 | tf_op jit(solution)/shard_map/while/body/eval_jaxpr/ppermute | solution.py:17
  327.7 9.4 %collective-permute-start.2 = (bf16[2,64,3,64]{3,1,2,0:T(8,128)(2,1)S(1)}, bf16[2,64,3,64]{3,1,2,0:T(8,128)(2,1)S(1)}, u32[]{:S(2)}, u32[]{:S(2)}) collective-permute-start(bf16[2,64,3,64]{3,1,2,0:T(8,128)(2,1)S(1)} %fusion.154), channel_id=1, source_target_pairs={{30,0},{0,2},{2,4},{4,6},{6,8},{8,10},{10,12},{12,14},{14,16},{16,... | collective-permute-start | bytes 147464 | tf_op jit(solution)/shard_map/while/body/eval_jaxpr/ppermute | solution.py:17
  328.1 10.3 %collective-permute-start.3 = (bf16[2,64,3,64]{3,1,2,0:T(8,128)(2,1)S(1)}, bf16[2,64,3,64]{3,1,2,0:T(8,128)(2,1)S(1)}, u32[]{:S(2)}, u32[]{:S(2)}) collective-permute-start(bf16[2,64,3,64]{3,1,2,0:T(8,128)(2,1)S(1)} %fusion.155), channel_id=1, source_target_pairs={{30,0},{0,2},{2,4},{4,6},{6,8},{8,10},{10,12},{12,14},{14,16},{16,... | collective-permute-start | bytes 147464 | tf_op jit(solution)/shard_map/while/body/eval_jaxpr/ppermute | solution.py:17
  338.4 13.9 %collective-permute-start = (bf16[2,64,3,64]{3,1,2,0:T(8,128)(2,1)S(1)}, bf16[2,64,3,64]{3,1,2,0:T(8,128)(2,1)S(1)}, u32[]{:S(2)}, u32[]{:S(2)}) collective-permute-start(bf16[2,64,3,64]{3,1,2,0:T(8,128)(2,1)S(1)} %copy.200), channel_id=1, source_target_pairs={{30,0},{0,2},{2,4},{4,6},{6,8},{8,10},{10,12},{12,14},{14,16},{16,... | collective-permute-start | bytes 147464 | tf_op jit(solution)/shard_map/while/body/eval_jaxpr/ppermute | solution.py:17
  338.5 13.9 %collective-permute-start.1 = (bf16[2,64,3,64]{3,1,2,0:T(8,128)(2,1)S(1)}, bf16[2,64,3,64]{3,1,2,0:T(8,128)(2,1)S(1)}, u32[]{:S(2)}, u32[]{:S(2)}) collective-permute-start(bf16[2,64,3,64]{3,1,2,0:T(8,128)(2,1)S(1)} %copy.201), channel_id=1, source_target_pairs={{30,0},{0,2},{2,4},{4,6},{6,8},{8,10},{10,12},{12,14},{14,16},{16,... | collective-permute-start | bytes 147464 | tf_op jit(solution)/shard_map/while/body/eval_jaxpr/ppermute | solution.py:17
  341.8 9.4 %collective-permute-start.2 = (bf16[2,64,3,64]{3,1,2,0:T(8,128)(2,1)S(1)}, bf16[2,64,3,64]{3,1,2,0:T(8,128)(2,1)S(1)}, u32[]{:S(2)}, u32[]{:S(2)}) collective-permute-start(bf16[2,64,3,64]{3,1,2,0:T(8,128)(2,1)S(1)} %fusion.154), channel_id=1, source_target_pairs={{30,0},{0,2},{2,4},{4,6},{6,8},{8,10},{10,12},{12,14},{14,16},{16,... | collective-permute-start | bytes 147464 | tf_op jit(solution)/shard_map/while/body/eval_jaxpr/ppermute | solution.py:17
  342.2 10.2 %collective-permute-start.3 = (bf16[2,64,3,64]{3,1,2,0:T(8,128)(2,1)S(1)}, bf16[2,64,3,64]{3,1,2,0:T(8,128)(2,1)S(1)}, u32[]{:S(2)}, u32[]{:S(2)}) collective-permute-start(bf16[2,64,3,64]{3,1,2,0:T(8,128)(2,1)S(1)} %fusion.155), channel_id=1, source_target_pairs={{30,0},{0,2},{2,4},{4,6},{6,8},{8,10},{10,12},{12,14},{14,16},{16,... | collective-permute-start | bytes 147464 | tf_op jit(solution)/shard_map/while/body/eval_jaxpr/ppermute | solution.py:17
  352.4 13.8 %collective-permute-start = (bf16[2,64,3,64]{3,1,2,0:T(8,128)(2,1)S(1)}, bf16[2,64,3,64]{3,1,2,0:T(8,128)(2,1)S(1)}, u32[]{:S(2)}, u32[]{:S(2)}) collective-permute-start(bf16[2,64,3,64]{3,1,2,0:T(8,128)(2,1)S(1)} %copy.200), channel_id=1, source_target_pairs={{30,0},{0,2},{2,4},{4,6},{6,8},{8,10},{10,12},{12,14},{14,16},{16,... | collective-permute-start | bytes 147464 | tf_op jit(solution)/shard_map/while/body/eval_jaxpr/ppermute | solution.py:17
  352.5 13.8 %collective-permute-start.1 = (bf16[2,64,3,64]{3,1,2,0:T(8,128)(2,1)S(1)}, bf16[2,64,3,64]{3,1,2,0:T(8,128)(2,1)S(1)}, u32[]{:S(2)}, u32[]{:S(2)}) collective-permute-start(bf16[2,64,3,64]{3,1,2,0:T(8,128)(2,1)S(1)} %copy.201), channel_id=1, source_target_pairs={{30,0},{0,2},{2,4},{4,6},{6,8},{8,10},{10,12},{12,14},{14,16},{16,... | collective-permute-start | bytes 147464 | tf_op jit(solution)/shard_map/while/body/eval_jaxpr/ppermute | solution.py:17
  355.8 9.4 %collective-permute-start.2 = (bf16[2,64,3,64]{3,1,2,0:T(8,128)(2,1)S(1)}, bf16[2,64,3,64]{3,1,2,0:T(8,128)(2,1)S(1)}, u32[]{:S(2)}, u32[]{:S(2)}) collective-permute-start(bf16[2,64,3,64]{3,1,2,0:T(8,128)(2,1)S(1)} %fusion.154), channel_id=1, source_target_pairs={{30,0},{0,2},{2,4},{4,6},{6,8},{8,10},{10,12},{12,14},{14,16},{16,... | collective-permute-start | bytes 147464 | tf_op jit(solution)/shard_map/while/body/eval_jaxpr/ppermute | solution.py:17
  356.2 10.1 %collective-permute-start.3 = (bf16[2,64,3,64]{3,1,2,0:T(8,128)(2,1)S(1)}, bf16[2,64,3,64]{3,1,2,0:T(8,128)(2,1)S(1)}, u32[]{:S(2)}, u32[]{:S(2)}) collective-permute-start(bf16[2,64,3,64]{3,1,2,0:T(8,128)(2,1)S(1)} %fusion.155), channel_id=1, source_target_pairs={{30,0},{0,2},{2,4},{4,6},{6,8},{8,10},{10,12},{12,14},{14,16},{16,... | collective-permute-start | bytes 147464 | tf_op jit(solution)/shard_map/while/body/eval_jaxpr/ppermute | solution.py:17
  366.3 13.0 %collective-permute-start = (bf16[2,64,3,64]{3,1,2,0:T(8,128)(2,1)S(1)}, bf16[2,64,3,64]{3,1,2,0:T(8,128)(2,1)S(1)}, u32[]{:S(2)}, u32[]{:S(2)}) collective-permute-start(bf16[2,64,3,64]{3,1,2,0:T(8,128)(2,1)S(1)} %copy.200), channel_id=1, source_target_pairs={{30,0},{0,2},{2,4},{4,6},{6,8},{8,10},{10,12},{12,14},{14,16},{16,... | collective-permute-start | bytes 147464 | tf_op jit(solution)/shard_map/while/body/eval_jaxpr/ppermute | solution.py:17
  366.4 13.0 %collective-permute-start.1 = (bf16[2,64,3,64]{3,1,2,0:T(8,128)(2,1)S(1)}, bf16[2,64,3,64]{3,1,2,0:T(8,128)(2,1)S(1)}, u32[]{:S(2)}, u32[]{:S(2)}) collective-permute-start(bf16[2,64,3,64]{3,1,2,0:T(8,128)(2,1)S(1)} %copy.201), channel_id=1, source_target_pairs={{30,0},{0,2},{2,4},{4,6},{6,8},{8,10},{10,12},{12,14},{14,16},{16,... | collective-permute-start | bytes 147464 | tf_op jit(solution)/shard_map/while/body/eval_jaxpr/ppermute | solution.py:17
  370.4 9.0 %collective-permute-start.3 = (bf16[2,64,3,64]{3,1,2,0:T(8,128)(2,1)S(1)}, bf16[2,64,3,64]{3,1,2,0:T(8,128)(2,1)S(1)}, u32[]{:S(2)}, u32[]{:S(2)}) collective-permute-start(bf16[2,64,3,64]{3,1,2,0:T(8,128)(2,1)S(1)} %fusion.155), channel_id=1, source_target_pairs={{30,0},{0,2},{2,4},{4,6},{6,8},{8,10},{10,12},{12,14},{14,16},{16,... | collective-permute-start | bytes 147464 | tf_op jit(solution)/shard_map/while/body/eval_jaxpr/ppermute | solution.py:17
  390.3 15.0 %reduce-scatter.10.cloned.1.call-start = ((), (), s32[]{:S(2)}) async-start(), calls=%async_computation.11 | async-start | bytes 442368 | tf_op jit(solution)/shard_map/reduce_scatter | solution.py:314
  391.7 25.1 %reduce-scatter.14.cloned.1.call-start = ((), (), s32[]{:S(2)}) async-start(), calls=%async_computation.13 | async-start | bytes 1105920 | tf_op jit(solution)/shard_map/reduce_scatter | solution.py:320
  393.0 36.0 %reduce-scatter.8.cloned.1.call-start = ((), (), s32[]{:S(2)}) async-start(), calls=%async_computation.10 | async-start | bytes 1105920 | tf_op jit(solution)/shard_map/reduce_scatter | solution.py:311
  395.5 46.8 %reduce-scatter.18.cloned.1.call-start = ((), (), s32[]{:S(2)}) async-start(), calls=%async_computation.15 | async-start | bytes 2654208 | tf_op jit(solution)/shard_map/reduce_scatter | solution.py:329
  397.5 58.3 %reduce-scatter.16.cloned.1.call-start = ((), (), s32[]{:S(2)}) async-start(), calls=%async_computation.14 | async-start | bytes 2654208 | tf_op jit(solution)/shard_map/reduce_scatter | solution.py:326
  399.4 69.6 %reduce-scatter.20.cloned.1.call-start = ((), (), s32[]{:S(2)}) async-start(), calls=%async_computation.16 | async-start | bytes 2654208 | tf_op jit(solution)/shard_map/reduce_scatter | solution.py:332
  401.3 238.7 %all-reduce.10.cloned.1.call-start = ((), (), s32[]{:S(2)}) async-start(), calls=%async_computation.17 | async-start | bytes 7372800 | tf_op jit(solution)/shard_map/psum | solution.py:340
  (60 other events, 643.9 us)
Sparse Core Ops, SparseCore 0:
  9.6 12.7 all-gather.3
  24.0 11.2 all-gather.5
  36.8 11.2 all-gather.7
  390.5 3.8 reduce-scatter.11
  396.4 8.8 reduce-scatter.9
  407.4 9.3 reduce-scatter.13
  419.6 9.3 reduce-scatter.7
  431.9 10.4 reduce-scatter.17
  445.3 10.4 reduce-scatter.15
  458.5 10.4 reduce-scatter.19
  476.6 163.4 all-reduce.9
where the time goes:
time: 657 us; the launch traced here: 655 us
  waiting for transfers between devices  310 us (47%)
  blocking collectives  162 us (25%)
  matrix products  68.4 us (10%)
  other arithmetic  44.1 us (7%)
  starting transfers between devices  41.7 us (6%)
  between operations  16.2 us (2%)
  local copies, waits for them, and re-layouts  10.6 us (2%)
    ppermute x62, waiting for transfers between devices, shifted(): return lax.ppermute(block, axis, route)  123 us
    psum x1, waiting for transfers between devices, local(): lax.psum(owned_grads[0].astype(jnp.bfloat16), 'ctx').astype(jnp.float32)  118 us
    all_gather x1, blocking collectives, local(): key_part = lax.all_gather(key_rows, 'ctx', axis=1, tiled=True)  54.9 us
    all_gather x1, blocking collectives, local(): value_part = lax.all_gather(value_rows, 'ctx', axis=1, tiled=True)  49.6 us
    psum x1, blocking collectives, local(): lax.psum(owned_grads[4].astype(jnp.bfloat16), 'ctx').astype(jnp.float32)  43.7 us
    ppermute x62, starting transfers between devices, shifted(): return lax.ppermute(block, axis, route)  41 us
    dot_general x16, matrix products, block_grads(): jnp.einsum('sqkgd,snkd->skgqn', queries, key_part, preferred_element_type...  17 us
    reduce_scatter x1, waiting for transfers between devices, local(): lax.psum_scatter(grad_wgate.astype(jnp.bfloat16), 'fsdp', scatter_dimensi...  13.4 us
  transfers between devices with their start and end apart: 73, of which 38 were waited for; matrix products, arithmetic and copies ran while one was open for 16% of the time, Pallas kernels for 0%

commit v1 on v0

--- a/solution.py
+++ b/solution.py
@@ -9,6 +9,16 @@
 epsilon = 1e-05
 theta_base = 100000.0
 masked_value = -1e30
+
+
+def pass_along(x, name, dim):
+    n_dev = lax.axis_size(name)
+    held, blocks = (x, [x])
+    for _ in range(n_dev - 1):
+        held = lax.ppermute(held, name, [(i, (i + 1) % n_dev) for i in range(n_dev)])
+        blocks.insert(0, held)
+    row_of_blocks = jnp.concatenate(blocks, axis=dim)
+    return jnp.roll(row_of_blocks, (lax.axis_index(name) + 1) * x.shape[dim], axis=dim)
 
 
 def shifted(block, axis, distance):
@@ -147,7 +157,7 @@
     stat_shape = (seq_count, KV_HEADS, group_size, tok_count)
     running_max = jnp.full(stat_shape, masked_value, jnp.float32)
     key_part = lax.all_gather(key_rows, "ctx", axis=1, tiled=True)
-    value_part = lax.all_gather(value_rows, "ctx", axis=1, tiled=True)
+    value_part = pass_along(value_rows, "ctx", 1)
     key_pos = slot_positions(block_of_slot, jnp.int32(0), key_part.shape[1], half_len)
     visible = query_pos[:, None] >= key_pos[None, :]
     scores = (

time: 657 us -> 717 us (1.091)
  waiting for transfers between devices: 310 us -> 401 us
  blocking collectives: 162 us -> 108 us
  starting transfers between devices: 41.7 us -> 57.8 us
  local copies, waits for them, and re-layouts: 10.6 us -> 18 us
    ppermute x0 -> x15, waiting for transfers between devices: none -> 105 us  [pass_along(): lax.ppermute(held, name, [(i, (i + 1) % n_dev) for i in range(n_dev)])]
    all_gather x1 -> x0, blocking collectives: 49.6 us -> none  [local(): value_part = lax.all_gather(value_rows, 'ctx', axis=1, tiled=True)]
    ppermute x62, waiting for transfers between devices: 123 us -> 109 us  [shifted(): return lax.ppermute(block, axis, route)]
    ppermute x62, starting transfers between devices: 41 us -> 54.1 us  [shifted(): return lax.ppermute(block, axis, route)]
  transfers between devices with their start and end apart: 73 -> 88, of which waited for: 38 -> 52; matrix products, arithmetic and copies ran while one was open for 16% -> 15% of each run, Pallas kernels for 0% -> 0%
where the time goes in v1:
time: 717 us; the launch traced here: 715 us
  waiting for transfers between devices  401 us (56%)
  blocking collectives  108 us (15%)
  matrix products  68.9 us (10%)
  starting transfers between devices  57.8 us (8%)
  other arithmetic  42.2 us (6%)
  local copies, waits for them, and re-layouts  18 us (3%)
  between operations  16.4 us (2%)
    psum x1, waiting for transfers between devices, local(): lax.psum(owned_grads[0].astype(jnp.bfloat16), 'ctx').astype(jnp.float32)  118 us
    ppermute x62, waiting for transfers between devices, shifted(): return lax.ppermute(block, axis, route)  109 us
    ppermute x15, waiting for transfers between devices, pass_along(): lax.ppermute(held, name, [(i, (i + 1) % n_dev) for i in range(n_dev)])  105 us
    ppermute x62, starting transfers between devices, shifted(): return lax.ppermute(block, axis, route)  54.1 us
    all_gather x1, blocking collectives, local(): key_part = lax.all_gather(key_rows, 'ctx', axis=1, tiled=True)  50.5 us
    psum x1, blocking collectives, local(): lax.psum(owned_grads[4].astype(jnp.bfloat16), 'ctx').astype(jnp.float32)  43.7 us
    dot_general x16, matrix products, block_grads(): jnp.einsum('sqkgd,snkd->skgqn', queries, key_part, preferred_element_type...  17 us
  transfers between devices with their start and end apart: 88, of which 52 were waited for; matrix products, arithmetic and copies ran while one was open for 15% of the time, Pallas kernels for 0%

profile of v1, /device:TPU:0, one launch (start us, length us, event | category | flops | bytes accessed | tf_op | source)
XLA Modules:
  0.0 714.6 jit_solution(2410887008916072973)
XLA Ops:
  10.6 2.6 all-reduce.7
  17.4 2.8 collective-permute-start.4
  25.6 50.5 %all_gather.32 = bf16[2,1024,3,64]{3,0,2,1:T(2,128)(2,1)S(1)} all-gather(bf16[2,64,3,64]{3,0,2,1:T(2,128)(2,1)S(1)} %copy.120), channel_id=1, replica_groups=mesh['ctx'=16,'fsdp'=2] {'ctx'}, dimensions={1}, use_global_device_ids=true | all-gather | bytes 835584 | tf_op jit(solution)/shard_map/all_gather | solution.py:159
  76.1 2.3 all_gather.33
  79.3 8.2 %collective-permute-done.5 = bf16[2,64,3,64]{1,3,2,0:T(8,128)(2,1)S(1)} collective-permute-done((bf16[2,64,3,64]{1,3,2,0:T(8,128)(2,1)}, bf16[2,64,3,64]{1,3,2,0:T(8,128)(2,1)S(1)}, u32[]{:S(2)}, u32[]{:S(2)}) %collective-permute-start.5) | collective-permute-done | bytes 49184 | tf_op jit(solution)/shard_map/ppermute | solution.py:18
  87.6 8.1 %collective-permute-done.6 = bf16[2,64,3,64]{1,3,2,0:T(8,128)(2,1)S(1)} collective-permute-done((bf16[2,64,3,64]{1,3,2,0:T(8,128)(2,1)S(1)}, bf16[2,64,3,64]{1,3,2,0:T(8,128)(2,1)S(1)}, u32[]{:S(2)}, u32[]{:S(2)}) %collective-permute-start.6) | collective-permute-done | bytes 49184 | tf_op jit(solution)/shard_map/ppermute | solution.py:18
  95.7 8.2 %collective-permute-done.7 = bf16[2,64,3,64]{1,3,2,0:T(8,128)(2,1)S(1)} collective-permute-done((bf16[2,64,3,64]{1,3,2,0:T(8,128)(2,1)S(1)}, bf16[2,64,3,64]{1,3,2,0:T(8,128)(2,1)S(1)}, u32[]{:S(2)}, u32[]{:S(2)}) %collective-permute-start.7) | collective-permute-done | bytes 49184 | tf_op jit(solution)/shard_map/ppermute | solution.py:18
  104.7 7.4 %collective-permute-done.8 = bf16[2,64,3,64]{1,3,2,0:T(8,128)(2,1)S(1)} collective-permute-done((bf16[2,64,3,64]{1,3,2,0:T(8,128)(2,1)S(1)}, bf16[2,64,3,64]{1,3,2,0:T(8,128)(2,1)S(1)}, u32[]{:S(2)}, u32[]{:S(2)}) %collective-permute-start.8) | collective-permute-done | bytes 49184 | tf_op jit(solution)/shard_map/ppermute | solution.py:18
  112.2 8.2 %collective-permute-done.9 = bf16[2,64,3,64]{1,3,2,0:T(8,128)(2,1)S(1)} collective-permute-done((bf16[2,64,3,64]{1,3,2,0:T(8,128)(2,1)S(1)}, bf16[2,64,3,64]{1,3,2,0:T(8,128)(2,1)S(1)}, u32[]{:S(2)}, u32[]{:S(2)}) %collective-permute-start.9) | collective-permute-done | bytes 49184 | tf_op jit(solution)/shard_map/ppermute | solution.py:18
  121.6 7.2 %collective-permute-done.10 = bf16[2,64,3,64]{1,3,2,0:T(8,128)(2,1)S(1)} collective-permute-done((bf16[2,64,3,64]{1,3,2,0:T(8,128)(2,1)S(1)}, bf16[2,64,3,64]{1,3,2,0:T(8,128)(2,1)S(1)}, u32[]{:S(2)}, u32[]{:S(2)}) %collective-permute-start.10) | collective-permute-done | bytes 49184 | tf_op jit(solution)/shard_map/ppermute | solution.py:18
  129.0 8.7 %collective-permute-done.11 = bf16[2,64,3,64]{1,3,2,0:T(8,128)(2,1)S(1)} collective-permute-done((bf16[2,64,3,64]{1,3,2,0:T(8,128)(2,1)S(1)}, bf16[2,64,3,64]{1,3,2,0:T(8,128)(2,1)S(1)}, u32[]{:S(2)}, u32[]{:S(2)}) %collective-permute-start.11) | collective-permute-done | bytes 49184 | tf_op jit(solution)/shard_map/ppermute | solution.py:18
  138.8 7.2 %collective-permute-done.12 = bf16[2,64,3,64]{1,3,2,0:T(8,128)(2,1)S(1)} collective-permute-done((bf16[2,64,3,64]{1,3,2,0:T(8,128)(2,1)S(1)}, bf16[2,64,3,64]{1,3,2,0:T(8,128)(2,1)S(1)}, u32[]{:S(2)}, u32[]{:S(2)}) %collective-permute-start.12) | collective-permute-done | bytes 49184 | tf_op jit(solution)/shard_map/ppermute | solution.py:18
  146.0 8.2 %collective-permute-done.13 = bf16[2,64,3,64]{1,3,2,0:T(8,128)(2,1)S(1)} collective-permute-done((bf16[2,64,3,64]{1,3,2,0:T(8,128)(2,1)S(1)}, bf16[2,64,3,64]{1,3,2,0:T(8,128)(2,1)S(1)}, u32[]{:S(2)}, u32[]{:S(2)}) %collective-permute-start.13) | collective-permute-done | bytes 49184 | tf_op jit(solution)/shard_map/ppermute | solution.py:18
  155.8 6.6 collective-permute-done.14
  163.0 7.6 %collective-permute-done.15 = bf16[2,64,3,64]{1,3,2,0:T(8,128)(2,1)S(1)} collective-permute-done((bf16[2,64,3,64]{1,3,2,0:T(8,128)(2,1)S(1)}, bf16[2,64,3,64]{1,3,2,0:T(8,128)(2,1)S(1)}, u32[]{:S(2)}, u32[]{:S(2)}) %collective-permute-start.15) | collective-permute-done | bytes 49184 | tf_op jit(solution)/shard_map/ppermute | solution.py:18
  170.6 8.2 %collective-permute-done.16 = bf16[2,64,3,64]{1,3,2,0:T(8,128)(2,1)S(1)} collective-permute-done((bf16[2,64,3,64]{1,3,2,0:T(8,128)(2,1)S(1)}, bf16[2,64,3,64]{1,3,2,0:T(8,128)(2,1)S(1)}, u32[]{:S(2)}, u32[]{:S(2)}) %collective-permute-start.16) | collective-permute-done | bytes 49184 | tf_op jit(solution)/shard_map/ppermute | solution.py:18
  180.2 7.0 collective-permute-done.17
  187.1 2.5 all_gather.35
  191.4 4.3 collective-permute-done.18
  195.7 6.4 concatenate.29
  202.1 5.0 fusion.42
  208.3 2.9 fusion.76
  211.2 2.9 fusion.77
  214.0 3.5 multiply_convert_fusion
  222.8 215.6 %while.25 = (s32[]{:T(128)}, bf16[2,64,3,64]{3,1,2,0:T(8,128)(2,1)S(1)}, bf16[2,64,3,64]{3,1,2,0:T(8,128)(2,1)S(1)}, f32[2,3,3,64,64]{4,3,2,1,0:T(8,128)S(1)}, f...) while((s32[]{:T(128)}, ...), condition=%wide.region_10.11_spmd.clone, body=%wide.region_8.10_spmd.clone.sunk | while | flops 48082768 | bytes 4246918 | solution.py:267
  227.0 7.5 %collective-permute-done.2 = bf16[2,64,3,64]{3,1,2,0:T(8,128)(2,1)S(1)} collective-permute-done((bf16[2,64,3,64]{3,1,2,0:T(8,128)(2,1)S(1)}, bf16[2,64,3,64]{3,1,2,0:T(8,128)(2,1)S(1)}, u32[]{:S(2)}, u32[]{:S(2)}) %collective-permute-start.2) | collective-permute-done | bytes 49184 | tf_op jit(solution)/shard_map/while/body/eval_jaxpr/ppermute | solution.py:27
  239.8 7.5 %collective-permute-done.2 = bf16[2,64,3,64]{3,1,2,0:T(8,128)(2,1)S(1)} collective-permute-done((bf16[2,64,3,64]{3,1,2,0:T(8,128)(2,1)S(1)}, bf16[2,64,3,64]{3,1,2,0:T(8,128)(2,1)S(1)}, u32[]{:S(2)}, u32[]{:S(2)}) %collective-permute-start.2) | collective-permute-done | bytes 49184 | tf_op jit(solution)/shard_map/while/body/eval_jaxpr/ppermute | solution.py:27
  252.6 7.5 %collective-permute-done.2 = bf16[2,64,3,64]{3,1,2,0:T(8,128)(2,1)S(1)} collective-permute-done((bf16[2,64,3,64]{3,1,2,0:T(8,128)(2,1)S(1)}, bf16[2,64,3,64]{3,1,2,0:T(8,128)(2,1)S(1)}, u32[]{:S(2)}, u32[]{:S(2)}) %collective-permute-start.2) | collective-permute-done | bytes 49184 | tf_op jit(solution)/shard_map/while/body/eval_jaxpr/ppermute | solution.py:27
  264.9 4.2 collective-permute-start.3
  269.4 3.4 collective-permute-done.2
  274.7 2.5 collective-permute-start.1
  280.5 2.4 collective-permute-start.2
  283.2 4.9 collective-permute-start.3
  293.4 3.4 collective-permute-start.1
  301.5 3.3 collective-permute-start.3
  305.1 3.5 collective-permute-done.2
  318.2 4.5 collective-permute-done.2
  330.6 5.8 collective-permute-done.2
  342.9 6.6 collective-permute-done.2
  355.5 7.7 %collective-permute-done.2 = bf16[2,64,3,64]{3,1,2,0:T(8,128)(2,1)S(1)} collective-permute-done((bf16[2,64,3,64]{3,1,2,0:T(8,128)(2,1)S(1)}, bf16[2,64,3,64]{3,1,2,0:T(8,128)(2,1)S(1)}, u32[]{:S(2)}, u32[]{:S(2)}) %collective-permute-start.2) | collective-permute-done | bytes 49184 | tf_op jit(solution)/shard_map/while/body/eval_jaxpr/ppermute | solution.py:27
  367.7 2.2 collective-permute-start.2
  370.1 4.0 collective-permute-start.3
  374.5 2.3 collective-permute-done.2
  383.8 2.4 collective-permute-start.2
  388.8 3.2 collective-permute-done.2
  392.1 2.7 collective-permute-done.3
  394.9 2.1 collective-permute-start.1
  400.8 3.2 collective-permute-start.3
  404.4 4.9 collective-permute-done.2
  409.3 2.1 collective-permute-done.3
  416.5 7.8 %collective-permute-done.2 = bf16[2,64,3,64]{3,1,2,0:T(8,128)(2,1)S(1)} collective-permute-done((bf16[2,64,3,64]{3,1,2,0:T(8,128)(2,1)S(1)}, bf16[2,64,3,64]{3,1,2,0:T(8,128)(2,1)S(1)}, u32[]{:S(2)}, u32[]{:S(2)}) %collective-permute-start.2) | collective-permute-done | bytes 49184 | tf_op jit(solution)/shard_map/while/body/eval_jaxpr/ppermute | solution.py:27
  429.8 7.4 %collective-permute-done.2 = bf16[2,64,3,64]{3,1,2,0:T(8,128)(2,1)S(1)} collective-permute-done((bf16[2,64,3,64]{3,1,2,0:T(8,128)(2,1)S(1)}, bf16[2,64,3,64]{3,1,2,0:T(8,128)(2,1)S(1)}, u32[]{:S(2)}, u32[]{:S(2)}) %collective-permute-start.2) | collective-permute-done | bytes 49184 | tf_op jit(solution)/shard_map/while/body/eval_jaxpr/ppermute | solution.py:27
  440.6 7.4 %collective-permute-done.20 = bf16[2,64,3,64]{1,3,2,0:T(8,128)(2,1)S(1)} collective-permute-done((bf16[2,64,3,64]{1,3,2,0:T(8,128)(2,1)S(1)}, bf16[2,64,3,64]{1,3,2,0:T(8,128)(2,1)S(1)}, u32[]{:S(2)}, u32[]{:S(2)}) %collective-permute-start.20) | collective-permute-done | bytes 49184 | tf_op jit(solution)/shard_map/ppermute | solution.py:27
  460.6 4.0 reduce-scatter.10.cloned.1.call-done
  464.6 11.5 %reduce-scatter.14.cloned.1.call-done = bf16[288,576]{1,0:T(8,128)(2,1)} async-done(((bf16[576,576]{1,0:T(8,128)(2,1)}), bf16[288,576]{1,0:T(8,128)(2,1)}) %reduce-scatter.14.cloned.1.call-update) | async-done | bytes 331792 | tf_op jit(solution)/shard_map/reduce_scatter | solution.py:330
  476.1 12.2 %reduce-scatter.8.cloned.1.call-done = bf16[288,576]{1,0:T(8,128)(2,1)} async-done(((bf16[576,576]{1,0:T(8,128)(2,1)}), bf16[288,576]{1,0:T(8,128)(2,1)}) %reduce-scatter.8.cloned.1.call-update) | async-done | bytes 331792 | tf_op jit(solution)/shard_map/reduce_scatter | solution.py:321
  488.3 13.3 %reduce-scatter.18.cloned.1.call-done = bf16[288,1536]{1,0:T(8,128)(2,1)} async-done(((bf16[576,1536]{1,0:T(8,128)(2,1)}), bf16[288,1536]{1,0:T(8,128)(2,1)}) %reduce-scatter.18.cloned.1.call-update) | async-done | bytes 884752 | tf_op jit(solution)/shard_map/reduce_scatter | solution.py:339
  501.7 13.4 %reduce-scatter.16.cloned.1.call-done = bf16[288,1536]{1,0:T(8,128)(2,1)} async-done(((bf16[576,1536]{1,0:T(8,128)(2,1)}), bf16[288,1536]{1,0:T(8,128)(2,1)}) %reduce-scatter.16.cloned.1.call-update) | async-done | bytes 884752 | tf_op jit(solution)/shard_map/reduce_scatter | solution.py:336
  515.1 13.2 %reduce-scatter.20.cloned.1.call-done = bf16[768,576]{0,1:T(8,128)(2,1)} async-done(((bf16[1536,576]{0,1:T(8,128)(2,1)}), bf16[768,576]{0,1:T(8,128)(2,1)}) %reduce-scatter.20.cloned.1.call-update) | async-done | bytes 884752 | tf_op jit(solution)/shard_map/reduce_scatter | solution.py:342
  529.0 2.1 fusion.32
  533.0 2.5 all-reduce.6
  535.6 43.7 %all-reduce.4 = (bf16[288]{0:T(512)(128)(2,1)S(1)}, bf16[288]{0:T(512)(128)(2,1)S(1)}) all-reduce(bf16[288]{0:T(512)(128)(2,1)S(1)} %dynamic-slice.3, bf16[288]{0:T(512)(128)(2,1)S(1)} %dynamic-slice.5), channel_id=1, replica_groups=mesh['ctx'=16,'fsdp'=2] {'ctx'}, use_global_device_ids=true, to_apply=%region_23.24 | all-reduce | flops 576 | bytes 2304 | tf_op jit(solution)/shard_map/psum | solution.py:354
  581.5 117.9 %all-reduce.10.cloned.1.call-done = (bf16[288,576]{1,0:T(8,128)(2,1)}, bf16[288,192]{1,0:T(8,128)(2,1)}, bf16[288,192]{1,0:T(8,128)(2,1)}, bf16[288,576]{1,0:T(8...) async-done(((bf16[288,576]{1,0:T(8,128)(2,1)}, bf16[288,192]{1,0:T(8,128)(2,1)}, bf16[288,192]{1,0:T(8,128)(2,1)}, ...) | async-done | bytes 3538960 | tf_op jit(solution)/shard_map/psum | solution.py:350
  699.3 2.7 convert_element_type.301
  (585 shorter events, 147.1 us)
Async XLA Ops:
  7.2 201.0 %all-gather.4.cloned.1.call-start = ((), (), s32[]{:S(2)}) async-start(), calls=%async_computation.7 | async-start | bytes 2654208 | tf_op jit(solution)/shard_map/all_gather | solution.py:110
  8.0 203.2 %all-gather.6.cloned.1.call-start = ((), (), s32[]{:S(2)}) async-start(), calls=%async_computation.8 | async-start | bytes 2654208 | tf_op jit(solution)/shard_map/all_gather | solution.py:111
  8.7 205.3 %all-gather.8.cloned.1.call-start = ((), (), s32[]{:S(2)}) async-start(), calls=%async_computation.9 | async-start | bytes 2654208 | tf_op jit(solution)/shard_map/all_gather | solution.py:112
  17.4 61.4 %collective-permute-start.4 = (bf16[2,64,3,64]{1,3,2,0:T(8,128)(2,1)}, bf16[2,64,3,64]{1,3,2,0:T(8,128)(2,1)}, u32[]{:S(2)}, u32[]{:S(2)}) collective-permute-start(bf16[2,64,3,64]{1,3,2,0:T(8,128)(2,1)} %copy.126), channel_id=1, source_target_pairs={{0,2},{2,4},{4,6},{6,8},{8,10},{10,12},{12,14},{14,16},{16,18},{18... | collective-permute-start | bytes 147464 | tf_op jit(solution)/shard_map/ppermute | solution.py:18
  20.2 440.4 %reduce-scatter.12.cloned.1.call-start = ((), (), s32[]{:S(2)}) async-start(), calls=%async_computation.12 | async-start | bytes 442368 | tf_op jit(solution)/shard_map/reduce_scatter | solution.py:327
  78.8 8.7 %collective-permute-start.5 = (bf16[2,64,3,64]{1,3,2,0:T(8,128)(2,1)}, bf16[2,64,3,64]{1,3,2,0:T(8,128)(2,1)S(1)}, u32[]{:S(2)}, u32[]{:S(2)}) collective-permute-start(bf16[2,64,3,64]{1,3,2,0:T(8,128)(2,1)} %collective-permute-done.4), channel_id=1, source_target_pairs={{0,2},{2,4},{4,6},{6,8},{8,10},{10,12},{12,14},{14,16},{16,18},{18... | collective-permute-start | bytes 147464 | tf_op jit(solution)/shard_map/ppermute | solution.py:18
  120.4 8.4 %collective-permute-start.10 = (bf16[2,64,3,64]{1,3,2,0:T(8,128)(2,1)S(1)}, bf16[2,64,3,64]{1,3,2,0:T(8,128)(2,1)S(1)}, u32[]{:S(2)}, u32[]{:S(2)}) collective-permute-start(bf16[2,64,3,64]{1,3,2,0:T(8,128)(2,1)S(1)} %collective-permute-done.9), channel_id=1, source_target_pairs={{0,2},{2,4},{4,6},{6,8},{8,10},{10,12},{12,14},{14,16},{16,18},{18... | collective-permute-start | bytes 147464 | tf_op jit(solution)/shard_map/ppermute | solution.py:18
  128.8 9.0 %collective-permute-start.11 = (bf16[2,64,3,64]{1,3,2,0:T(8,128)(2,1)S(1)}, bf16[2,64,3,64]{1,3,2,0:T(8,128)(2,1)S(1)}, u32[]{:S(2)}, u32[]{:S(2)}) collective-permute-start(bf16[2,64,3,64]{1,3,2,0:T(8,128)(2,1)S(1)} %collective-permute-done.10), channel_id=1, source_target_pairs={{0,2},{2,4},{4,6},{6,8},{8,10},{10,12},{12,14},{14,16},{16,18},{18... | collective-permute-start | bytes 147464 | tf_op jit(solution)/shard_map/ppermute | solution.py:18
  187.1 8.5 %collective-permute-start.18 = (bf16[2,64,3,64]{1,3,2,0:T(8,128)(2,1)}, bf16[2,64,3,64]{1,3,2,0:T(8,128)(2,1)}, u32[]{:S(2)}, u32[]{:S(2)}) collective-permute-start(bf16[2,64,3,64]{1,3,2,0:T(8,128)(2,1)} %collective-permute-done.17), channel_id=1, source_target_pairs={{0,2},{2,4},{4,6},{6,8},{8,10},{10,12},{12,14},{14,16},{16,18},{18... | collective-permute-start | bytes 147464 | tf_op jit(solution)/shard_map/ppermute | solution.py:18
  222.8 12.7 %collective-permute-start = (bf16[2,64,3,64]{3,1,2,0:T(8,128)(2,1)S(1)}, bf16[2,64,3,64]{3,1,2,0:T(8,128)(2,1)S(1)}, u32[]{:S(2)}, u32[]{:S(2)}) collective-permute-start(bf16[2,64,3,64]{3,1,2,0:T(8,128)(2,1)S(1)} %copy.200), channel_id=1, source_target_pairs={{30,0},{0,2},{2,4},{4,6},{6,8},{8,10},{10,12},{12,14},{14,16},{16,... | collective-permute-start | bytes 147464 | tf_op jit(solution)/shard_map/while/body/eval_jaxpr/ppermute | solution.py:27
  222.9 12.7 %collective-permute-start.1 = (bf16[2,64,3,64]{3,1,2,0:T(8,128)(2,1)S(1)}, bf16[2,64,3,64]{3,1,2,0:T(8,128)(2,1)S(1)}, u32[]{:S(2)}, u32[]{:S(2)}) collective-permute-start(bf16[2,64,3,64]{3,1,2,0:T(8,128)(2,1)S(1)} %copy.201), channel_id=1, source_target_pairs={{30,0},{0,2},{2,4},{4,6},{6,8},{8,10},{10,12},{12,14},{14,16},{16,... | collective-permute-start | bytes 147464 | tf_op jit(solution)/shard_map/while/body/eval_jaxpr/ppermute | solution.py:27
  226.6 9.0 %collective-permute-start.3 = (bf16[2,64,3,64]{3,1,2,0:T(8,128)(2,1)S(1)}, bf16[2,64,3,64]{3,1,2,0:T(8,128)(2,1)S(1)}, u32[]{:S(2)}, u32[]{:S(2)}) collective-permute-start(bf16[2,64,3,64]{3,1,2,0:T(8,128)(2,1)S(1)} %fusion.157), channel_id=1, source_target_pairs={{30,0},{0,2},{2,4},{4,6},{6,8},{8,10},{10,12},{12,14},{14,16},{16,... | collective-permute-start | bytes 147464 | tf_op jit(solution)/shard_map/while/body/eval_jaxpr/ppermute | solution.py:27
  235.6 12.7 %collective-permute-start = (bf16[2,64,3,64]{3,1,2,0:T(8,128)(2,1)S(1)}, bf16[2,64,3,64]{3,1,2,0:T(8,128)(2,1)S(1)}, u32[]{:S(2)}, u32[]{:S(2)}) collective-permute-start(bf16[2,64,3,64]{3,1,2,0:T(8,128)(2,1)S(1)} %copy.200), channel_id=1, source_target_pairs={{30,0},{0,2},{2,4},{4,6},{6,8},{8,10},{10,12},{12,14},{14,16},{16,... | collective-permute-start | bytes 147464 | tf_op jit(solution)/shard_map/while/body/eval_jaxpr/ppermute | solution.py:27
  235.7 12.7 %collective-permute-start.1 = (bf16[2,64,3,64]{3,1,2,0:T(8,128)(2,1)S(1)}, bf16[2,64,3,64]{3,1,2,0:T(8,128)(2,1)S(1)}, u32[]{:S(2)}, u32[]{:S(2)}) collective-permute-start(bf16[2,64,3,64]{3,1,2,0:T(8,128)(2,1)S(1)} %copy.201), channel_id=1, source_target_pairs={{30,0},{0,2},{2,4},{4,6},{6,8},{8,10},{10,12},{12,14},{14,16},{16,... | collective-permute-start | bytes 147464 | tf_op jit(solution)/shard_map/while/body/eval_jaxpr/ppermute | solution.py:27
  239.3 9.0 %collective-permute-start.3 = (bf16[2,64,3,64]{3,1,2,0:T(8,128)(2,1)S(1)}, bf16[2,64,3,64]{3,1,2,0:T(8,128)(2,1)S(1)}, u32[]{:S(2)}, u32[]{:S(2)}) collective-permute-start(bf16[2,64,3,64]{3,1,2,0:T(8,128)(2,1)S(1)} %fusion.157), channel_id=1, source_target_pairs={{30,0},{0,2},{2,4},{4,6},{6,8},{8,10},{10,12},{12,14},{14,16},{16,... | collective-permute-start | bytes 147464 | tf_op jit(solution)/shard_map/while/body/eval_jaxpr/ppermute | solution.py:27
  248.4 12.7 %collective-permute-start = (bf16[2,64,3,64]{3,1,2,0:T(8,128)(2,1)S(1)}, bf16[2,64,3,64]{3,1,2,0:T(8,128)(2,1)S(1)}, u32[]{:S(2)}, u32[]{:S(2)}) collective-permute-start(bf16[2,64,3,64]{3,1,2,0:T(8,128)(2,1)S(1)} %copy.200), channel_id=1, source_target_pairs={{30,0},{0,2},{2,4},{4,6},{6,8},{8,10},{10,12},{12,14},{14,16},{16,... | collective-permute-start | bytes 147464 | tf_op jit(solution)/shard_map/while/body/eval_jaxpr/ppermute | solution.py:27
  248.5 12.7 %collective-permute-start.1 = (bf16[2,64,3,64]{3,1,2,0:T(8,128)(2,1)S(1)}, bf16[2,64,3,64]{3,1,2,0:T(8,128)(2,1)S(1)}, u32[]{:S(2)}, u32[]{:S(2)}) collective-permute-start(bf16[2,64,3,64]{3,1,2,0:T(8,128)(2,1)S(1)} %copy.201), channel_id=1, source_target_pairs={{30,0},{0,2},{2,4},{4,6},{6,8},{8,10},{10,12},{12,14},{14,16},{16,... | collective-permute-start | bytes 147464 | tf_op jit(solution)/shard_map/while/body/eval_jaxpr/ppermute | solution.py:27
  252.1 9.0 %collective-permute-start.3 = (bf16[2,64,3,64]{3,1,2,0:T(8,128)(2,1)S(1)}, bf16[2,64,3,64]{3,1,2,0:T(8,128)(2,1)S(1)}, u32[]{:S(2)}, u32[]{:S(2)}) collective-permute-start(bf16[2,64,3,64]{3,1,2,0:T(8,128)(2,1)S(1)} %fusion.157), channel_id=1, source_target_pairs={{30,0},{0,2},{2,4},{4,6},{6,8},{8,10},{10,12},{12,14},{14,16},{16,... | collective-permute-start | bytes 147464 | tf_op jit(solution)/shard_map/while/body/eval_jaxpr/ppermute | solution.py:27
  261.2 13.4 %collective-permute-start = (bf16[2,64,3,64]{3,1,2,0:T(8,128)(2,1)S(1)}, bf16[2,64,3,64]{3,1,2,0:T(8,128)(2,1)S(1)}, u32[]{:S(2)}, u32[]{:S(2)}) collective-permute-start(bf16[2,64,3,64]{3,1,2,0:T(8,128)(2,1)S(1)} %copy.200), channel_id=1, source_target_pairs={{30,0},{0,2},{2,4},{4,6},{6,8},{8,10},{10,12},{12,14},{14,16},{16,... | collective-permute-start | bytes 147464 | tf_op jit(solution)/shard_map/while/body/eval_jaxpr/ppermute | solution.py:27
  261.3 13.3 %collective-permute-start.1 = (bf16[2,64,3,64]{3,1,2,0:T(8,128)(2,1)S(1)}, bf16[2,64,3,64]{3,1,2,0:T(8,128)(2,1)S(1)}, u32[]{:S(2)}, u32[]{:S(2)}) collective-permute-start(bf16[2,64,3,64]{3,1,2,0:T(8,128)(2,1)S(1)} %copy.201), channel_id=1, source_target_pairs={{30,0},{0,2},{2,4},{4,6},{6,8},{8,10},{10,12},{12,14},{14,16},{16,... | collective-permute-start | bytes 147464 | tf_op jit(solution)/shard_map/while/body/eval_jaxpr/ppermute | solution.py:27
  264.9 9.6 %collective-permute-start.3 = (bf16[2,64,3,64]{3,1,2,0:T(8,128)(2,1)S(1)}, bf16[2,64,3,64]{3,1,2,0:T(8,128)(2,1)S(1)}, u32[]{:S(2)}, u32[]{:S(2)}) collective-permute-start(bf16[2,64,3,64]{3,1,2,0:T(8,128)(2,1)S(1)} %fusion.157), channel_id=1, source_target_pairs={{30,0},{0,2},{2,4},{4,6},{6,8},{8,10},{10,12},{12,14},{14,16},{16,... | collective-permute-start | bytes 147464 | tf_op jit(solution)/shard_map/while/body/eval_jaxpr/ppermute | solution.py:27
  274.6 16.8 %collective-permute-start = (bf16[2,64,3,64]{3,1,2,0:T(8,128)(2,1)S(1)}, bf16[2,64,3,64]{3,1,2,0:T(8,128)(2,1)S(1)}, u32[]{:S(2)}, u32[]{:S(2)}) collective-permute-start(bf16[2,64,3,64]{3,1,2,0:T(8,128)(2,1)S(1)} %copy.200), channel_id=1, source_target_pairs={{30,0},{0,2},{2,4},{4,6},{6,8},{8,10},{10,12},{12,14},{14,16},{16,... | collective-permute-start | bytes 147464 | tf_op jit(solution)/shard_map/while/body/eval_jaxpr/ppermute | solution.py:27
  274.7 16.7 %collective-permute-start.1 = (bf16[2,64,3,64]{3,1,2,0:T(8,128)(2,1)S(1)}, bf16[2,64,3,64]{3,1,2,0:T(8,128)(2,1)S(1)}, u32[]{:S(2)}, u32[]{:S(2)}) collective-permute-start(bf16[2,64,3,64]{3,1,2,0:T(8,128)(2,1)S(1)} %copy.201), channel_id=1, source_target_pairs={{30,0},{0,2},{2,4},{4,6},{6,8},{8,10},{10,12},{12,14},{14,16},{16,... | collective-permute-start | bytes 147464 | tf_op jit(solution)/shard_map/while/body/eval_jaxpr/ppermute | solution.py:27
  280.5 9.3 %collective-permute-start.2 = (bf16[2,64,3,64]{3,1,2,0:T(8,128)(2,1)S(1)}, bf16[2,64,3,64]{3,1,2,0:T(8,128)(2,1)S(1)}, u32[]{:S(2)}, u32[]{:S(2)}) collective-permute-start(bf16[2,64,3,64]{3,1,2,0:T(8,128)(2,1)S(1)} %fusion.156), channel_id=1, source_target_pairs={{30,0},{0,2},{2,4},{4,6},{6,8},{8,10},{10,12},{12,14},{14,16},{16,... | collective-permute-start | bytes 147464 | tf_op jit(solution)/shard_map/while/body/eval_jaxpr/ppermute | solution.py:27
  291.5 18.3 %collective-permute-start = (bf16[2,64,3,64]{3,1,2,0:T(8,128)(2,1)S(1)}, bf16[2,64,3,64]{3,1,2,0:T(8,128)(2,1)S(1)}, u32[]{:S(2)}, u32[]{:S(2)}) collective-permute-start(bf16[2,64,3,64]{3,1,2,0:T(8,128)(2,1)S(1)} %copy.200), channel_id=1, source_target_pairs={{30,0},{0,2},{2,4},{4,6},{6,8},{8,10},{10,12},{12,14},{14,16},{16,... | collective-permute-start | bytes 147464 | tf_op jit(solution)/shard_map/while/body/eval_jaxpr/ppermute | solution.py:27
  293.4 16.4 %collective-permute-start.1 = (bf16[2,64,3,64]{3,1,2,0:T(8,128)(2,1)S(1)}, bf16[2,64,3,64]{3,1,2,0:T(8,128)(2,1)S(1)}, u32[]{:S(2)}, u32[]{:S(2)}) collective-permute-start(bf16[2,64,3,64]{3,1,2,0:T(8,128)(2,1)S(1)} %copy.201), channel_id=1, source_target_pairs={{30,0},{0,2},{2,4},{4,6},{6,8},{8,10},{10,12},{12,14},{14,16},{16,... | collective-permute-start | bytes 147464 | tf_op jit(solution)/shard_map/while/body/eval_jaxpr/ppermute | solution.py:27
  300.1 8.5 %collective-permute-start.2 = (bf16[2,64,3,64]{3,1,2,0:T(8,128)(2,1)S(1)}, bf16[2,64,3,64]{3,1,2,0:T(8,128)(2,1)S(1)}, u32[]{:S(2)}, u32[]{:S(2)}) collective-permute-start(bf16[2,64,3,64]{3,1,2,0:T(8,128)(2,1)S(1)} %fusion.156), channel_id=1, source_target_pairs={{30,0},{0,2},{2,4},{4,6},{6,8},{8,10},{10,12},{12,14},{14,16},{16,... | collective-permute-start | bytes 147464 | tf_op jit(solution)/shard_map/while/body/eval_jaxpr/ppermute | solution.py:27
  309.9 14.3 %collective-permute-start = (bf16[2,64,3,64]{3,1,2,0:T(8,128)(2,1)S(1)}, bf16[2,64,3,64]{3,1,2,0:T(8,128)(2,1)S(1)}, u32[]{:S(2)}, u32[]{:S(2)}) collective-permute-start(bf16[2,64,3,64]{3,1,2,0:T(8,128)(2,1)S(1)} %copy.200), channel_id=1, source_target_pairs={{30,0},{0,2},{2,4},{4,6},{6,8},{8,10},{10,12},{12,14},{14,16},{16,... | collective-permute-start | bytes 147464 | tf_op jit(solution)/shard_map/while/body/eval_jaxpr/ppermute | solution.py:27
  309.9 14.3 %collective-permute-start.1 = (bf16[2,64,3,64]{3,1,2,0:T(8,128)(2,1)S(1)}, bf16[2,64,3,64]{3,1,2,0:T(8,128)(2,1)S(1)}, u32[]{:S(2)}, u32[]{:S(2)}) collective-permute-start(bf16[2,64,3,64]{3,1,2,0:T(8,128)(2,1)S(1)} %copy.201), channel_id=1, source_target_pairs={{30,0},{0,2},{2,4},{4,6},{6,8},{8,10},{10,12},{12,14},{14,16},{16,... | collective-permute-start | bytes 147464 | tf_op jit(solution)/shard_map/while/body/eval_jaxpr/ppermute | solution.py:27
  324.3 13.1 %collective-permute-start = (bf16[2,64,3,64]{3,1,2,0:T(8,128)(2,1)S(1)}, bf16[2,64,3,64]{3,1,2,0:T(8,128)(2,1)S(1)}, u32[]{:S(2)}, u32[]{:S(2)}) collective-permute-start(bf16[2,64,3,64]{3,1,2,0:T(8,128)(2,1)S(1)} %copy.200), channel_id=1, source_target_pairs={{30,0},{0,2},{2,4},{4,6},{6,8},{8,10},{10,12},{12,14},{14,16},{16,... | collective-permute-start | bytes 147464 | tf_op jit(solution)/shard_map/while/body/eval_jaxpr/ppermute | solution.py:27
  324.3 13.1 %collective-permute-start.1 = (bf16[2,64,3,64]{3,1,2,0:T(8,128)(2,1)S(1)}, bf16[2,64,3,64]{3,1,2,0:T(8,128)(2,1)S(1)}, u32[]{:S(2)}, u32[]{:S(2)}) collective-permute-start(bf16[2,64,3,64]{3,1,2,0:T(8,128)(2,1)S(1)} %copy.201), channel_id=1, source_target_pairs={{30,0},{0,2},{2,4},{4,6},{6,8},{8,10},{10,12},{12,14},{14,16},{16,... | collective-permute-start | bytes 147464 | tf_op jit(solution)/shard_map/while/body/eval_jaxpr/ppermute | solution.py:27
  328.4 8.9 %collective-permute-start.3 = (bf16[2,64,3,64]{3,1,2,0:T(8,128)(2,1)S(1)}, bf16[2,64,3,64]{3,1,2,0:T(8,128)(2,1)S(1)}, u32[]{:S(2)}, u32[]{:S(2)}) collective-permute-start(bf16[2,64,3,64]{3,1,2,0:T(8,128)(2,1)S(1)} %fusion.157), channel_id=1, source_target_pairs={{30,0},{0,2},{2,4},{4,6},{6,8},{8,10},{10,12},{12,14},{14,16},{16,... | collective-permute-start | bytes 147464 | tf_op jit(solution)/shard_map/while/body/eval_jaxpr/ppermute | solution.py:27
  337.5 13.1 %collective-permute-start = (bf16[2,64,3,64]{3,1,2,0:T(8,128)(2,1)S(1)}, bf16[2,64,3,64]{3,1,2,0:T(8,128)(2,1)S(1)}, u32[]{:S(2)}, u32[]{:S(2)}) collective-permute-start(bf16[2,64,3,64]{3,1,2,0:T(8,128)(2,1)S(1)} %copy.200), channel_id=1, source_target_pairs={{30,0},{0,2},{2,4},{4,6},{6,8},{8,10},{10,12},{12,14},{14,16},{16,... | collective-permute-start | bytes 147464 | tf_op jit(solution)/shard_map/while/body/eval_jaxpr/ppermute | solution.py:27
  337.5 13.1 %collective-permute-start.1 = (bf16[2,64,3,64]{3,1,2,0:T(8,128)(2,1)S(1)}, bf16[2,64,3,64]{3,1,2,0:T(8,128)(2,1)S(1)}, u32[]{:S(2)}, u32[]{:S(2)}) collective-permute-start(bf16[2,64,3,64]{3,1,2,0:T(8,128)(2,1)S(1)} %copy.201), channel_id=1, source_target_pairs={{30,0},{0,2},{2,4},{4,6},{6,8},{8,10},{10,12},{12,14},{14,16},{16,... | collective-permute-start | bytes 147464 | tf_op jit(solution)/shard_map/while/body/eval_jaxpr/ppermute | solution.py:27
  340.9 8.7 %collective-permute-start.2 = (bf16[2,64,3,64]{3,1,2,0:T(8,128)(2,1)S(1)}, bf16[2,64,3,64]{3,1,2,0:T(8,128)(2,1)S(1)}, u32[]{:S(2)}, u32[]{:S(2)}) collective-permute-start(bf16[2,64,3,64]{3,1,2,0:T(8,128)(2,1)S(1)} %fusion.156), channel_id=1, source_target_pairs={{30,0},{0,2},{2,4},{4,6},{6,8},{8,10},{10,12},{12,14},{14,16},{16,... | collective-permute-start | bytes 147464 | tf_op jit(solution)/shard_map/while/body/eval_jaxpr/ppermute | solution.py:27
  341.2 9.4 %collective-permute-start.3 = (bf16[2,64,3,64]{3,1,2,0:T(8,128)(2,1)S(1)}, bf16[2,64,3,64]{3,1,2,0:T(8,128)(2,1)S(1)}, u32[]{:S(2)}, u32[]{:S(2)}) collective-permute-start(bf16[2,64,3,64]{3,1,2,0:T(8,128)(2,1)S(1)} %fusion.157), channel_id=1, source_target_pairs={{30,0},{0,2},{2,4},{4,6},{6,8},{8,10},{10,12},{12,14},{14,16},{16,... | collective-permute-start | bytes 147464 | tf_op jit(solution)/shard_map/while/body/eval_jaxpr/ppermute | solution.py:27
  350.7 13.6 %collective-permute-start = (bf16[2,64,3,64]{3,1,2,0:T(8,128)(2,1)S(1)}, bf16[2,64,3,64]{3,1,2,0:T(8,128)(2,1)S(1)}, u32[]{:S(2)}, u32[]{:S(2)}) collective-permute-start(bf16[2,64,3,64]{3,1,2,0:T(8,128)(2,1)S(1)} %copy.200), channel_id=1, source_target_pairs={{30,0},{0,2},{2,4},{4,6},{6,8},{8,10},{10,12},{12,14},{14,16},{16,... | collective-permute-start | bytes 147464 | tf_op jit(solution)/shard_map/while/body/eval_jaxpr/ppermute | solution.py:27
  350.7 13.5 %collective-permute-start.1 = (bf16[2,64,3,64]{3,1,2,0:T(8,128)(2,1)S(1)}, bf16[2,64,3,64]{3,1,2,0:T(8,128)(2,1)S(1)}, u32[]{:S(2)}, u32[]{:S(2)}) collective-permute-start(bf16[2,64,3,64]{3,1,2,0:T(8,128)(2,1)S(1)} %copy.201), channel_id=1, source_target_pairs={{30,0},{0,2},{2,4},{4,6},{6,8},{8,10},{10,12},{12,14},{14,16},{16,... | collective-permute-start | bytes 147464 | tf_op jit(solution)/shard_map/while/body/eval_jaxpr/ppermute | solution.py:27
  354.1 9.1 %collective-permute-start.2 = (bf16[2,64,3,64]{3,1,2,0:T(8,128)(2,1)S(1)}, bf16[2,64,3,64]{3,1,2,0:T(8,128)(2,1)S(1)}, u32[]{:S(2)}, u32[]{:S(2)}) collective-permute-start(bf16[2,64,3,64]{3,1,2,0:T(8,128)(2,1)S(1)} %fusion.156), channel_id=1, source_target_pairs={{30,0},{0,2},{2,4},{4,6},{6,8},{8,10},{10,12},{12,14},{14,16},{16,... | collective-permute-start | bytes 147464 | tf_op jit(solution)/shard_map/while/body/eval_jaxpr/ppermute | solution.py:27
  354.4 9.8 %collective-permute-start.3 = (bf16[2,64,3,64]{3,1,2,0:T(8,128)(2,1)S(1)}, bf16[2,64,3,64]{3,1,2,0:T(8,128)(2,1)S(1)}, u32[]{:S(2)}, u32[]{:S(2)}) collective-permute-start(bf16[2,64,3,64]{3,1,2,0:T(8,128)(2,1)S(1)} %fusion.157), channel_id=1, source_target_pairs={{30,0},{0,2},{2,4},{4,6},{6,8},{8,10},{10,12},{12,14},{14,16},{16,... | collective-permute-start | bytes 147464 | tf_op jit(solution)/shard_map/while/body/eval_jaxpr/ppermute | solution.py:27
  364.3 14.1 %collective-permute-start = (bf16[2,64,3,64]{3,1,2,0:T(8,128)(2,1)S(1)}, bf16[2,64,3,64]{3,1,2,0:T(8,128)(2,1)S(1)}, u32[]{:S(2)}, u32[]{:S(2)}) collective-permute-start(bf16[2,64,3,64]{3,1,2,0:T(8,128)(2,1)S(1)} %copy.200), channel_id=1, source_target_pairs={{30,0},{0,2},{2,4},{4,6},{6,8},{8,10},{10,12},{12,14},{14,16},{16,... | collective-permute-start | bytes 147464 | tf_op jit(solution)/shard_map/while/body/eval_jaxpr/ppermute | solution.py:27
  364.3 14.1 %collective-permute-start.1 = (bf16[2,64,3,64]{3,1,2,0:T(8,128)(2,1)S(1)}, bf16[2,64,3,64]{3,1,2,0:T(8,128)(2,1)S(1)}, u32[]{:S(2)}, u32[]{:S(2)}) collective-permute-start(bf16[2,64,3,64]{3,1,2,0:T(8,128)(2,1)S(1)} %copy.201), channel_id=1, source_target_pairs={{30,0},{0,2},{2,4},{4,6},{6,8},{8,10},{10,12},{12,14},{14,16},{16,... | collective-permute-start | bytes 147464 | tf_op jit(solution)/shard_map/while/body/eval_jaxpr/ppermute | solution.py:27
  367.7 9.1 %collective-permute-start.2 = (bf16[2,64,3,64]{3,1,2,0:T(8,128)(2,1)S(1)}, bf16[2,64,3,64]{3,1,2,0:T(8,128)(2,1)S(1)}, u32[]{:S(2)}, u32[]{:S(2)}) collective-permute-start(bf16[2,64,3,64]{3,1,2,0:T(8,128)(2,1)S(1)} %fusion.156), channel_id=1, source_target_pairs={{30,0},{0,2},{2,4},{4,6},{6,8},{8,10},{10,12},{12,14},{14,16},{16,... | collective-permute-start | bytes 147464 | tf_op jit(solution)/shard_map/while/body/eval_jaxpr/ppermute | solution.py:27
  378.4 16.3 %collective-permute-start = (bf16[2,64,3,64]{3,1,2,0:T(8,128)(2,1)S(1)}, bf16[2,64,3,64]{3,1,2,0:T(8,128)(2,1)S(1)}, u32[]{:S(2)}, u32[]{:S(2)}) collective-permute-start(bf16[2,64,3,64]{3,1,2,0:T(8,128)(2,1)S(1)} %copy.200), channel_id=1, source_target_pairs={{30,0},{0,2},{2,4},{4,6},{6,8},{8,10},{10,12},{12,14},{14,16},{16,... | collective-permute-start | bytes 147464 | tf_op jit(solution)/shard_map/while/body/eval_jaxpr/ppermute | solution.py:27
  378.9 15.9 %collective-permute-start.1 = (bf16[2,64,3,64]{3,1,2,0:T(8,128)(2,1)S(1)}, bf16[2,64,3,64]{3,1,2,0:T(8,128)(2,1)S(1)}, u32[]{:S(2)}, u32[]{:S(2)}) collective-permute-start(bf16[2,64,3,64]{3,1,2,0:T(8,128)(2,1)S(1)} %copy.201), channel_id=1, source_target_pairs={{30,0},{0,2},{2,4},{4,6},{6,8},{8,10},{10,12},{12,14},{14,16},{16,... | collective-permute-start | bytes 147464 | tf_op jit(solution)/shard_map/while/body/eval_jaxpr/ppermute | solution.py:27
  394.8 16.6 %collective-permute-start = (bf16[2,64,3,64]{3,1,2,0:T(8,128)(2,1)S(1)}, bf16[2,64,3,64]{3,1,2,0:T(8,128)(2,1)S(1)}, u32[]{:S(2)}, u32[]{:S(2)}) collective-permute-start(bf16[2,64,3,64]{3,1,2,0:T(8,128)(2,1)S(1)} %copy.200), channel_id=1, source_target_pairs={{30,0},{0,2},{2,4},{4,6},{6,8},{8,10},{10,12},{12,14},{14,16},{16,... | collective-permute-start | bytes 147464 | tf_op jit(solution)/shard_map/while/body/eval_jaxpr/ppermute | solution.py:27
  394.9 16.5 %collective-permute-start.1 = (bf16[2,64,3,64]{3,1,2,0:T(8,128)(2,1)S(1)}, bf16[2,64,3,64]{3,1,2,0:T(8,128)(2,1)S(1)}, u32[]{:S(2)}, u32[]{:S(2)}) collective-permute-start(bf16[2,64,3,64]{3,1,2,0:T(8,128)(2,1)S(1)} %copy.201), channel_id=1, source_target_pairs={{30,0},{0,2},{2,4},{4,6},{6,8},{8,10},{10,12},{12,14},{14,16},{16,... | collective-permute-start | bytes 147464 | tf_op jit(solution)/shard_map/while/body/eval_jaxpr/ppermute | solution.py:27
  400.2 9.1 %collective-permute-start.2 = (bf16[2,64,3,64]{3,1,2,0:T(8,128)(2,1)S(1)}, bf16[2,64,3,64]{3,1,2,0:T(8,128)(2,1)S(1)}, u32[]{:S(2)}, u32[]{:S(2)}) collective-permute-start(bf16[2,64,3,64]{3,1,2,0:T(8,128)(2,1)S(1)} %fusion.156), channel_id=1, source_target_pairs={{30,0},{0,2},{2,4},{4,6},{6,8},{8,10},{10,12},{12,14},{14,16},{16,... | collective-permute-start | bytes 147464 | tf_op jit(solution)/shard_map/while/body/eval_jaxpr/ppermute | solution.py:27
  400.8 10.6 %collective-permute-start.3 = (bf16[2,64,3,64]{3,1,2,0:T(8,128)(2,1)S(1)}, bf16[2,64,3,64]{3,1,2,0:T(8,128)(2,1)S(1)}, u32[]{:S(2)}, u32[]{:S(2)}) collective-permute-start(bf16[2,64,3,64]{3,1,2,0:T(8,128)(2,1)S(1)} %fusion.157), channel_id=1, source_target_pairs={{30,0},{0,2},{2,4},{4,6},{6,8},{8,10},{10,12},{12,14},{14,16},{16,... | collective-permute-start | bytes 147464 | tf_op jit(solution)/shard_map/while/body/eval_jaxpr/ppermute | solution.py:27
  411.4 14.1 %collective-permute-start = (bf16[2,64,3,64]{3,1,2,0:T(8,128)(2,1)S(1)}, bf16[2,64,3,64]{3,1,2,0:T(8,128)(2,1)S(1)}, u32[]{:S(2)}, u32[]{:S(2)}) collective-permute-start(bf16[2,64,3,64]{3,1,2,0:T(8,128)(2,1)S(1)} %copy.200), channel_id=1, source_target_pairs={{30,0},{0,2},{2,4},{4,6},{6,8},{8,10},{10,12},{12,14},{14,16},{16,... | collective-permute-start | bytes 147464 | tf_op jit(solution)/shard_map/while/body/eval_jaxpr/ppermute | solution.py:27
  411.5 14.0 %collective-permute-start.1 = (bf16[2,64,3,64]{3,1,2,0:T(8,128)(2,1)S(1)}, bf16[2,64,3,64]{3,1,2,0:T(8,128)(2,1)S(1)}, u32[]{:S(2)}, u32[]{:S(2)}) collective-permute-start(bf16[2,64,3,64]{3,1,2,0:T(8,128)(2,1)S(1)} %copy.201), channel_id=1, source_target_pairs={{30,0},{0,2},{2,4},{4,6},{6,8},{8,10},{10,12},{12,14},{14,16},{16,... | collective-permute-start | bytes 147464 | tf_op jit(solution)/shard_map/while/body/eval_jaxpr/ppermute | solution.py:27
  415.0 9.3 %collective-permute-start.2 = (bf16[2,64,3,64]{3,1,2,0:T(8,128)(2,1)S(1)}, bf16[2,64,3,64]{3,1,2,0:T(8,128)(2,1)S(1)}, u32[]{:S(2)}, u32[]{:S(2)}) collective-permute-start(bf16[2,64,3,64]{3,1,2,0:T(8,128)(2,1)S(1)} %fusion.156), channel_id=1, source_target_pairs={{30,0},{0,2},{2,4},{4,6},{6,8},{8,10},{10,12},{12,14},{14,16},{16,... | collective-permute-start | bytes 147464 | tf_op jit(solution)/shard_map/while/body/eval_jaxpr/ppermute | solution.py:27
  415.3 10.2 %collective-permute-start.3 = (bf16[2,64,3,64]{3,1,2,0:T(8,128)(2,1)S(1)}, bf16[2,64,3,64]{3,1,2,0:T(8,128)(2,1)S(1)}, u32[]{:S(2)}, u32[]{:S(2)}) collective-permute-start(bf16[2,64,3,64]{3,1,2,0:T(8,128)(2,1)S(1)} %fusion.157), channel_id=1, source_target_pairs={{30,0},{0,2},{2,4},{4,6},{6,8},{8,10},{10,12},{12,14},{14,16},{16,... | collective-permute-start | bytes 147464 | tf_op jit(solution)/shard_map/while/body/eval_jaxpr/ppermute | solution.py:27
  425.6 12.7 %collective-permute-start = (bf16[2,64,3,64]{3,1,2,0:T(8,128)(2,1)S(1)}, bf16[2,64,3,64]{3,1,2,0:T(8,128)(2,1)S(1)}, u32[]{:S(2)}, u32[]{:S(2)}) collective-permute-start(bf16[2,64,3,64]{3,1,2,0:T(8,128)(2,1)S(1)} %copy.200), channel_id=1, source_target_pairs={{30,0},{0,2},{2,4},{4,6},{6,8},{8,10},{10,12},{12,14},{14,16},{16,... | collective-permute-start | bytes 147464 | tf_op jit(solution)/shard_map/while/body/eval_jaxpr/ppermute | solution.py:27
  425.7 12.7 %collective-permute-start.1 = (bf16[2,64,3,64]{3,1,2,0:T(8,128)(2,1)S(1)}, bf16[2,64,3,64]{3,1,2,0:T(8,128)(2,1)S(1)}, u32[]{:S(2)}, u32[]{:S(2)}) collective-permute-start(bf16[2,64,3,64]{3,1,2,0:T(8,128)(2,1)S(1)} %copy.201), channel_id=1, source_target_pairs={{30,0},{0,2},{2,4},{4,6},{6,8},{8,10},{10,12},{12,14},{14,16},{16,... | collective-permute-start | bytes 147464 | tf_op jit(solution)/shard_map/while/body/eval_jaxpr/ppermute | solution.py:27
  429.3 9.0 %collective-permute-start.3 = (bf16[2,64,3,64]{3,1,2,0:T(8,128)(2,1)S(1)}, bf16[2,64,3,64]{3,1,2,0:T(8,128)(2,1)S(1)}, u32[]{:S(2)}, u32[]{:S(2)}) collective-permute-start(bf16[2,64,3,64]{3,1,2,0:T(8,128)(2,1)S(1)} %fusion.157), channel_id=1, source_target_pairs={{30,0},{0,2},{2,4},{4,6},{6,8},{8,10},{10,12},{12,14},{14,16},{16,... | collective-permute-start | bytes 147464 | tf_op jit(solution)/shard_map/while/body/eval_jaxpr/ppermute | solution.py:27
  440.6 8.8 %collective-permute-start.19 = (bf16[2,64,3,64]{1,3,2,0:T(8,128)(2,1)S(1)}, bf16[2,64,3,64]{1,3,2,0:T(8,128)(2,1)S(1)}, u32[]{:S(2)}, u32[]{:S(2)}) collective-permute-start(bf16[2,64,3,64]{1,3,2,0:T(8,128)(2,1)S(1)} %fusion.38), channel_id=1, source_target_pairs={{30,0},{0,2},{2,4},{4,6},{6,8},{8,10},{10,12},{12,14},{14,16},{16,... | collective-permute-start | bytes 147464 | tf_op jit(solution)/shard_map/ppermute | solution.py:27
  449.3 15.3 %reduce-scatter.10.cloned.1.call-start = ((), (), s32[]{:S(2)}) async-start(), calls=%async_computation.11 | async-start | bytes 442368 | tf_op jit(solution)/shard_map/reduce_scatter | solution.py:324
  450.7 25.4 %reduce-scatter.14.cloned.1.call-start = ((), (), s32[]{:S(2)}) async-start(), calls=%async_computation.13 | async-start | bytes 1105920 | tf_op jit(solution)/shard_map/reduce_scatter | solution.py:330
  452.0 36.3 %reduce-scatter.8.cloned.1.call-start = ((), (), s32[]{:S(2)}) async-start(), calls=%async_computation.10 | async-start | bytes 1105920 | tf_op jit(solution)/shard_map/reduce_scatter | solution.py:321
  454.5 47.1 %reduce-scatter.18.cloned.1.call-start = ((), (), s32[]{:S(2)}) async-start(), calls=%async_computation.15 | async-start | bytes 2654208 | tf_op jit(solution)/shard_map/reduce_scatter | solution.py:339
  456.7 58.4 %reduce-scatter.16.cloned.1.call-start = ((), (), s32[]{:S(2)}) async-start(), calls=%async_computation.14 | async-start | bytes 2654208 | tf_op jit(solution)/shard_map/reduce_scatter | solution.py:336
  458.6 69.7 %reduce-scatter.20.cloned.1.call-start = ((), (), s32[]{:S(2)}) async-start(), calls=%async_computation.16 | async-start | bytes 2654208 | tf_op jit(solution)/shard_map/reduce_scatter | solution.py:342
  460.5 238.8 %all-reduce.10.cloned.1.call-start = ((), (), s32[]{:S(2)}) async-start(), calls=%async_computation.17 | async-start | bytes 7372800 | tf_op jit(solution)/shard_map/psum | solution.py:350
  (98 other events, 1338.4 us)
Sparse Core Ops, SparseCore 0:
  9.6 12.7 all-gather.3
  24.0 11.2 all-gather.5
  36.8 11.2 all-gather.7
  449.4 4.1 reduce-scatter.11
  455.7 8.8 reduce-scatter.9
  466.7 9.3 reduce-scatter.13
  479.0 9.3 reduce-scatter.7
  491.2 10.4 reduce-scatter.17
  504.6 10.4 reduce-scatter.15
  517.8 10.4 reduce-scatter.19
  535.8 163.4 all-reduce.9
